TPU v7x, 32 devices: a whole 2x2x4 slice. The times are simulated.
32 devices in a mesh: dom: 8 (over z, y), sub: 4 (over x, core).
Axes of the slice: x: 2, y: 2, z: 4, core: 2. Of those that a mesh axis runs over, the one named last changes fastest.
Arguments:
- displacement: float32 [3, 128, 289], P(None, ('dom', 'sub')), may hold values from -6 to 6
- macro_modulus: float32 [8, 32768], P(None, ('dom', 'sub')), may hold values from 0.5 to 4
- damaged_count: int32 [32], P(('dom', 'sub')), may hold values from 1 to 64, 1024 in all
- damaged_points: int32 [32, 64], P(('dom', 'sub')), may hold values from 0 to 8191, as said below
- damage: bfloat16 [2048, 4096], P(('dom', 'sub')), may hold values from 0 to 0.59765625
- voxel_modulus: bfloat16 [2048, 4096], P(('dom', 'sub')), may hold values from 0.5 to 4
Outputs:
- nodal_force: float32 [3, 128, 289], P(None, ('dom', 'sub'))
- new_damage: bfloat16 [2048, 4096], P(('dom', 'sub'))
Inputs may be any that keep to these rules, and one draw needn't show every extreme that they name: `damaged_count`: the counts of all partitions sum to 1024, and the largest is 64. `damaged_points`: each row names 64 different points of its partition; the first damaged_count of them are the damaged ones; partition 0 lists point 0 and point 8 * 4 * 16^2 - 1.
All inputs are finite; a program needn't handle non-finite values. No bound on the sum of `damaged_count` on one device may be relied on, other than what follows from the above.
Results may differ from a plain program's by a relative error of at most 0.0055.
Values may be sent and summed in bfloat16 or wider, within the bound.
A program may use at most 64 MiB of HBM per device.

v0:
```python
import math

import jax
import jax.numpy as jnp
import numpy as np
from jax import lax
from jax.experimental import pallas as pl
from jax.experimental.pallas import tpu as pltpu
from jax.sharding import PartitionSpec as P

CELL = 16
PLANE = CELL * CELL
VOX = CELL**3
EXY = 16
NODES = (EXY + 1) ** 2
NODE_PAD = 384
HALF = 128
ROWS = 16

lam_hat = 0.2 / 0.72
mu_hat = 1.0 / 2.4
ref_modulus = 2.0
kappa_sq = 4.0
voigt_pairs = ((0, 0), (1, 1), (2, 2), (1, 2), (0, 2), (0, 1))
packed = {}
for _a in range(6):
    for _b in range(_a, 6):
        packed[(_a, _b)] = packed[(_b, _a)] = len(packed) - sum(
            1 for _p in packed if _p[0] > _p[1]
        )
C1, C2, C3 = (math.cos(math.pi * n / 8) for n in (1, 2, 3))
f32, bf16 = jnp.float32, jnp.bfloat16
HIGHEST = lax.Precision.HIGHEST


def shifted(value, axis, steps):
    count = lax.axis_size(axis)
    initial, last = (max(0, -steps), min(count, count - steps))
    return lax.ppermute(value, axis, [(source, source + steps) for source in range(initial, last)])


def shape_table():
    gauss_coord = 1.0 / math.sqrt(3.0)
    gradients = np.zeros((8, 8, 3))
    for corner in range(8):
        signs = [2 * (corner >> d & 1) - 1 for d in range(3)]
        for gauss_no in range(8):
            coords = [(2 * (gauss_no >> d & 1) - 1) * gauss_coord for d in range(3)]
            factor = [(1.0 + signs[d] * coords[d]) / 2.0 for d in range(3)]
            for d in range(3):
                value = float(signs[d])
                for other in range(3):
                    if other != d:
                        value *= factor[other]
                gradients[corner, gauss_no, d] = value
    return gradients


def macro_tables():
    table = shape_table()
    to_strain = np.zeros((48, 32))
    to_force = np.zeros((32, 48))
    for corner in range(8):
        base = (corner & 3) * 8 + (corner >> 2) * 3
        for k, (a, b) in enumerate(voigt_pairs):
            for q in range(8):
                to_strain[k * 8 + q, base + a] += 0.5 * table[corner, q, b]
                to_strain[k * 8 + q, base + b] += 0.5 * table[corner, q, a]
                to_force[base + a, k * 8 + q] += 0.125 * table[corner, q, b]
                if a != b:
                    to_force[base + b, k * 8 + q] += 0.125 * table[corner, q, a]
    pick = np.zeros((NODE_PAD, 4 * EXY * EXY))
    for cy in range(2):
        for cx in range(2):
            for y in range(EXY):
                for x in range(EXY):
                    column = (2 * cy + cx) * EXY * EXY + y * EXY + x
                    pick[(y + cy) * (EXY + 1) + x + cx, column] = 1.0
    return to_strain, to_force, pick


def green_matrix(nx, ny, nz):
    n = np.stack(np.broadcast_arrays(nx, ny, nz)).astype(np.float64)
    square = (n * n).sum(0)
    inverse = np.where(square > 0.5, 1.0 / np.maximum(square, 1.0), 0.0)
    lam_ref, mu_ref = ref_modulus * lam_hat, ref_modulus * mu_hat
    coupling = (lam_ref + mu_ref) / (mu_ref * (lam_ref + 2.0 * mu_ref))
    out = np.zeros((6, 6) + square.shape)
    for column, (a, b) in enumerate(voigt_pairs):
        traction = np.zeros_like(n)
        traction[a] += n[b]
        if a != b:
            traction[b] += n[a]
        along = (n * traction).sum(0)
        amplitude = inverse * traction / mu_ref - coupling * along * inverse * inverse * n
        for k, (c, d) in enumerate(voigt_pairs):
            out[k, column] = 0.5 * (n[c] * amplitude[d] + n[d] * amplitude[c])
    return out


def effective_green():
    index = np.arange(CELL)
    signed = np.where(index < CELL // 2, index, index - CELL)
    mirror = (-index) % CELL
    half = CELL // 2
    fx, fy = signed[:, None, None], signed[None, :, None]
    given = green_matrix(fx, fy, np.arange(half + 1)[None, None, :])
    turned = given[:, :, mirror][:, :, :, mirror]
    full = np.zeros((6, 6, CELL, CELL, CELL))
    full[..., : half + 1] = given
    for plane in (0, half):
        full[..., plane] = 0.5 * (given[..., plane] + turned[..., plane])
    for plane in range(half + 1, CELL):
        full[..., plane] = turned[..., CELL - plane]
    full[:, 3:] *= 0.5
    return full[:, :, : half + 1].reshape(6, 6, half + 1, PLANE)


def cell_tables():
    green = effective_green()
    coefs = np.zeros((9, 24, PLANE))
    for a in range(6):
        for b in range(a, 6):
            coefs[:, packed[(a, b)]] = green[a, b]
    wide = green.transpose(2, 1, 0, 3).reshape(9, 6, 6 * PLANE)
    upper = wide.astype(bf16).astype(np.float64)
    first = np.zeros((9, 32, 6 * PLANE))
    first[:, 0:6] = upper
    first[:, 6:12] = upper
    first[:, 12:18] = wide - upper
    place = np.arange(PLANE)
    phase = (place // CELL)[:, None] * (place // CELL)[None, :] + (place % CELL)[:, None] * (
        place % CELL
    )[None, :]
    angle = (phase % CELL) * (2.0 * math.pi / CELL)
    cos, sin = np.cos(angle), np.sin(angle)
    forward = np.block([[cos, sin], [-sin, cos]])
    inverse = np.block([[cos, -sin], [sin, cos]]) * (2.0 / VOX)
    return coefs, first, forward, inverse, cos + sin, (cos + sin) / VOX


def parts3(value):
    first = value.astype(bf16)
    rest = value - first.astype(f32)
    second = rest.astype(bf16)
    third = (rest - second.astype(f32)).astype(bf16)
    return jnp.concatenate([first, second, third], axis=0)


def total3(value):
    rows = value.shape[0] // 3
    return value[:rows] + value[rows : 2 * rows] + value[2 * rows :]


def forward_x(v):
    s = [v[x] + v[x + 8] for x in range(8)]
    d = [v[x] - v[x + 8] for x in range(8)]
    a = [s[x] + s[x + 4] for x in range(4)]
    b = [s[x] - s[x + 4] for x in range(4)]
    a02, a13 = a[0] + a[2], a[1] + a[3]
    bm, bp = C2 * (b[1] - b[3]), C2 * (b[1] + b[3])
    p1, p2, p3 = d[1] - d[7], C2 * (d[2] - d[6]), d[3] - d[5]
    q1, q2, q3 = d[1] + d[7], C2 * (d[2] + d[6]), d[3] + d[5]
    re_sum, re_dif = d[0] + p2, d[0] - p2
    re_a, re_b = C1 * p1 + C3 * p3, C3 * p1 - C1 * p3
    im_sum, im_dif = q2 + d[4], q2 - d[4]
    im_a, im_b = C3 * q1 + C1 * q3, C1 * q1 - C3 * q3
    pairs = [
        (re_sum + re_a, im_a + im_sum),
        (b[0] + bm, bp + b[2]),
        (re_dif + re_b, im_b + im_dif),
        (a[0] - a[2], a[1] - a[3]),
        (re_dif - re_b, im_b - im_dif),
        (b[0] - bm, bp - b[2]),
        (re_sum - re_a, im_a - im_sum),
    ]
    return a02 + a13, a02 - a13, pairs


def inverse_x(x0, x8, pairs):
    r = [None] + [pair[0] for pair in pairs]
    m = [None] + [pair[1] for pair in pairs]
    plus, minus = x0 + x8, x0 - x8
    r26p, r26m = r[2] + r[6], C2 * (r[2] - r[6])
    p4 = plus + r[4]
    even = [p4 + r26p, minus + r26m, plus - r[4], minus - r26m, p4 - r26p]
    r17p, r17m, r35p, r35m = r[1] + r[7], r[1] - r[7], r[3] + r[5], r[3] - r[5]
    odd = [r17p + r35p, C1 * r17m + C3 * r35m, C2 * (r17p - r35p), C3 * r17m - C1 * r35m]
    cosine = [None] * 9
    for x in range(4):
        cosine[x] = even[x] + odd[x]
        cosine[8 - x] = even[x] - odd[x]
    cosine[4] = even[4]
    m26p = C2 * (m[2] + m[6])
    s_even = [None, m26p + m[4], m[2] - m[6], m26p - m[4]]
    m17p, m17m, m35p, m35m = m[1] + m[7], m[1] - m[7], m[3] + m[5], m[3] - m[5]
    s_odd = [None, C3 * m17p + C1 * m35p, C2 * (m17m + m35m), C1 * m17p - C3 * m35p]
    sine = [None] * 8
    for x in range(1, 4):
        sine[x] = s_odd[x] + s_even[x]
        sine[8 - x] = s_odd[x] - s_even[x]
    sine[4] = m17m - m35m
    out = [None] * 16
    out[0], out[8] = cosine[0], cosine[8]
    for x in range(1, 8):
        out[x] = cosine[x] + sine[x]
        out[16 - x] = cosine[x] - sine[x]
    return out


def damage_of(e):
    energy = e[0] * e[0] + e[1] * e[1] + e[2] * e[2]
    energy = energy + 2.0 * (e[3] * e[3] + e[4] * e[4] + e[5] * e[5])
    return energy / (energy + kappa_sq)


def unit_law(e, shear):
    volume = lam_hat * (e[0] + e[1] + e[2])
    return [2.0 * mu_hat * e[k] + volume for k in range(3)] + [
        (shear * 2.0 * mu_hat) * e[k] for k in range(3, 6)
    ]


def kernel(
    layers,
    slots,
    count_ref,
    nodes_ref,
    modulus_ref,
    points_ref,
    damage_ref,
    voxel_ref,
    strain_tab,
    force_tab,
    pick_tab,
    coef_tab,
    first_tab,
    forward_tab,
    inverse_tab,
    real_forward,
    real_inverse,
    force_ref,
    new_ref,
    field,
    spec_c,
    spec_r,
    back_c,
    back_r,
    freq,
    green,
    macro,
    stress_s,
    acc,
):
    elems = layers * EXY * EXY
    chunks = slots // ROWS
    count = count_ref[0]

    spread = total3(jnp.dot(parts3(nodes_ref[...]), pick_tab[...], preferred_element_type=f32))
    plane = EXY * EXY
    corners = jnp.concatenate(
        [
            jnp.concatenate(
                [spread[z * 8 : z * 8 + 8, c * plane : (c + 1) * plane] for z in range(layers)],
                axis=1,
            )
            for c in range(4)
        ],
        axis=0,
    )
    strain = jnp.dot(strain_tab[...], corners, precision=HIGHEST, preferred_element_type=f32)
    modulus = modulus_ref[...]
    law = unit_law([strain[k * 8 : k * 8 + 8] for k in range(6)], 1.0)
    stress = jnp.concatenate([modulus * law[k] for k in range(6)], axis=0)
    stress_s[...] = stress

    points = points_ref[...]
    element = points % elems
    gauss = points // elems
    hot = (lax.broadcasted_iota(jnp.int32, (slots, elems), 1) == element).astype(f32).astype(bf16)
    both = parts3(jnp.concatenate([strain, stress], axis=0))
    picked = lax.dot_general(hot, both, (((1,), (1,)), ((), ())), preferred_element_type=f32)
    picked = picked[:, 0:96] + picked[:, 96:192] + picked[:, 192:288]
    lane96 = lax.broadcasted_iota(jnp.int32, (slots, 96), 1)
    own = [
        jnp.sum(jnp.where(lane96 == k * 8 + gauss, picked, 0.0), axis=1, keepdims=True)
        for k in range(12)
    ]
    mean = [own[k].astype(bf16).astype(f32) for k in range(6)]
    for k in range(6):
        macro[k] = jnp.broadcast_to(mean[k], (slots, HALF))

    mean_law = unit_law(mean, 2.0)
    mean_damage = damage_of(mean)
    lane32 = lax.broadcasted_iota(jnp.int32, (slots, 32), 1)
    upper = jnp.zeros((slots, 32), f32)
    for k in range(6):
        high = mean_law[k].astype(bf16).astype(f32)
        upper = jnp.where((lane32 == k) | (lane32 == 12 + k), high, upper)
        upper = jnp.where(lane32 == 6 + k, mean_law[k] - high, upper)
    mean_parts = upper.astype(bf16)
    for r in range(chunks):
        rows = slice(r * ROWS, (r + 1) * ROWS)
        for h in range(2):
            lanes = slice(h * HALF, (h + 1) * HALF)
            scalar = []
            for x in range(CELL):
                cols = slice(x * PLANE + h * HALF, x * PLANE + (h + 1) * HALF)
                old = damage_ref[rows, cols].astype(f32)
                young = voxel_ref[rows, cols].astype(f32)
                scalar.append((1.0 - jnp.maximum(old, mean_damage[rows])) * young - ref_modulus)
            x0, x8, pairs = forward_x(scalar)
            spec_r[0, rows, lanes] = x0.astype(bf16)
            spec_r[1, rows, lanes] = x8.astype(bf16)
            for j in range(7):
                spec_c[j, rows, h * HALF : (h + 1) * HALF] = pairs[j][0].astype(bf16)
                spec_c[j, rows, PLANE + h * HALF : PLANE + (h + 1) * HALF] = pairs[j][1].astype(
                    bf16
                )

    def first_c(j, carry):
        spectrum = jnp.dot(spec_c[j, 0:slots], forward_tab[...], preferred_element_type=f32)
        weight = jnp.dot(mean_parts, first_tab[j + 1], preferred_element_type=f32)
        for k in range(6):
            part = weight[:, k * PLANE : (k + 1) * PLANE]
            rows = slice(k * slots, (k + 1) * slots)
            green[rows, 0:PLANE] = (part * spectrum[:, 0:PLANE]).astype(bf16)
            green[rows, PLANE:] = (part * spectrum[:, PLANE:]).astype(bf16)
        back_c[j] = jnp.dot(green[...], inverse_tab[...], preferred_element_type=f32)
        return carry

    def first_r(j, carry):
        spectrum = jnp.dot(spec_r[j, 0:slots], real_forward[...], preferred_element_type=f32)
        weight = jnp.dot(mean_parts, first_tab[j * 8], preferred_element_type=f32)
        for k in range(6):
            part = weight[:, k * PLANE : (k + 1) * PLANE]
            green[k * slots : (k + 1) * slots, 0:PLANE] = (part * spectrum).astype(bf16)
        back_r[j] = jnp.dot(green[:, 0:PLANE], real_inverse[...], preferred_element_type=f32)
        return carry

    def to_strain(k, carry):
        for r in range(chunks):
            rows = pl.ds(pl.multiple_of(k * slots + r * ROWS, ROWS), ROWS)
            base = macro[k, r * ROWS : (r + 1) * ROWS]
            for h in range(2):
                lanes = slice(h * HALF, (h + 1) * HALF)
                upper_lanes = slice(PLANE + h * HALF, PLANE + (h + 1) * HALF)
                pairs = [(back_c[j, rows, lanes], back_c[j, rows, upper_lanes]) for j in range(7)]
                values = inverse_x(back_r[0, rows, lanes], back_r[1, rows, lanes], pairs)
                for x in range(CELL):
                    field[k * CELL + x, r * ROWS : (r + 1) * ROWS, lanes] = base - values[x]
        return carry

    lax.fori_loop(0, 7, first_c, 0)
    lax.fori_loop(0, 2, first_r, 0)
    lax.fori_loop(0, 6, to_strain, 0)

    def polarize(x, carry):
        cols = pl.ds(pl.multiple_of(x * PLANE, PLANE), PLANE)
        for r in range(chunks):
            rows = slice(r * ROWS, (r + 1) * ROWS)
            e = [field[k * CELL + x, rows] for k in range(6)]
            old = damage_ref[rows, cols].astype(f32)
            young = voxel_ref[rows, cols].astype(f32)
            change = (1.0 - jnp.maximum(old, damage_of(e))) * young - ref_modulus
            for k, unit in enumerate(unit_law(e, 2.0)):
                field[k * CELL + x, rows] = change * unit
        return carry

    def to_spectrum(k, carry):
        for r in range(chunks):
            rows = pl.ds(pl.multiple_of(k * slots + r * ROWS, ROWS), ROWS)
            for h in range(2):
                lanes = slice(h * HALF, (h + 1) * HALF)
                upper_lanes = slice(PLANE + h * HALF, PLANE + (h + 1) * HALF)
                x0, x8, pairs = forward_x(
                    [field[k * CELL + x, r * ROWS : (r + 1) * ROWS, lanes] for x in range(CELL)]
                )
                spec_r[0, rows, lanes] = x0.astype(bf16)
                spec_r[1, rows, lanes] = x8.astype(bf16)
                for j in range(7):
                    spec_c[j, rows, lanes] = pairs[j][0].astype(bf16)
                    spec_c[j, rows, upper_lanes] = pairs[j][1].astype(bf16)
        return carry

    def apply_green(index, planes):
        for h in range(2):
            lanes = slice(h * HALF, (h + 1) * HALF)
            coefs = [
                jnp.broadcast_to(coef_tab[index, c : c + 1, lanes], (ROWS, HALF))
                for c in range(21)
            ]
            for part in range(planes):
                where = slice(part * PLANE + h * HALF, part * PLANE + (h + 1) * HALF)
                for r in range(chunks):
                    t = [
                        freq[k * slots + r * ROWS : k * slots + (r + 1) * ROWS, where]
                        for k in range(6)
                    ]
                    for k in range(6):
                        total = coefs[packed[(k, 0)]] * t[0]
                        for b in range(1, 6):
                            total = total + coefs[packed[(k, b)]] * t[b]
                        green[k * slots + r * ROWS : k * slots + (r + 1) * ROWS, where] = (
                            total.astype(bf16)
                        )

    def second_c(j, carry):
        freq[...] = jnp.dot(spec_c[j], forward_tab[...], preferred_element_type=f32)
        apply_green(j + 1, 2)
        back_c[j] = jnp.dot(green[...], inverse_tab[...], preferred_element_type=f32)
        return carry

    def second_r(j, carry):
        freq[:, 0:PLANE] = jnp.dot(spec_r[j], real_forward[...], preferred_element_type=f32)
        apply_green(j * 8, 1)
        back_r[j] = jnp.dot(green[:, 0:PLANE], real_inverse[...], preferred_element_type=f32)
        return carry

    lax.fori_loop(0, CELL, polarize, 0)
    lax.fori_loop(0, 6, to_spectrum, 0)
    lax.fori_loop(0, 7, second_c, 0)
    lax.fori_loop(0, 2, second_r, 0)
    lax.fori_loop(0, 6, to_strain, 0)

    for r in range(chunks):
        rows = slice(r * ROWS, (r + 1) * ROWS)
        live = lax.broadcasted_iota(jnp.int32, (ROWS, PLANE), 0) + r * ROWS < count

        def finish(x, sums, rows=rows, live=live):
            cols = pl.ds(pl.multiple_of(x * PLANE, PLANE), PLANE)
            e = [field[k * CELL + x, rows] for k in range(6)]
            old = damage_ref[rows, cols].astype(f32)
            young = voxel_ref[rows, cols].astype(f32)
            now = jnp.maximum(old, damage_of(e))
            new_ref[rows, cols] = jnp.where(live, now, old).astype(bf16)
            left = (1.0 - now) * young
            out = []
            for k, unit in enumerate(unit_law(e, 1.0)):
                value = left * unit
                out.append(sums[k] + (value[:, 0:HALF] + value[:, HALF:]))
            return tuple(out)

        sums = lax.fori_loop(0, CELL, finish, (jnp.zeros((ROWS, HALF), f32),) * 6)
        for k in range(6):
            acc[k, rows] = sums[k]

    alive = lax.broadcasted_iota(jnp.int32, (slots, 1), 0) < count
    lane128 = lax.broadcasted_iota(jnp.int32, (slots, HALF), 1)
    change = jnp.zeros((slots, HALF), f32)
    for k in range(6):
        cell_mean = jnp.sum(acc[k], axis=1, keepdims=True) * (1.0 / VOX)
        delta = jnp.where(alive, cell_mean.astype(bf16).astype(f32) - own[6 + k], 0.0)
        change = jnp.where(lane128 == k * 8 + gauss, delta, change)
    turned = jnp.transpose(change)[0:48]
    stress = stress_s[...] + total3(jnp.dot(parts3(turned), hot, preferred_element_type=f32))
    contrib = jnp.dot(force_tab[...], stress, precision=HIGHEST, preferred_element_type=f32)
    by_layer = jnp.concatenate(
        [
            jnp.concatenate(
                [contrib[c * 8 : c * 8 + 8, z * plane : (z + 1) * plane] for c in range(4)], axis=1
            )
            for z in range(layers)
        ],
        axis=0,
    )
    force_ref[...] = total3(
        lax.dot_general(
            parts3(by_layer), pick_tab[...], (((1,), (1,)), ((), ())), preferred_element_type=f32
        )
    )


def run_kernel(count, nodes, modulus, points, damage, voxel, layers, interpret=False):
    slots = damage.shape[0]
    to_strain, to_force, pick = macro_tables()
    coefs, first, forward, inverse, real_forward, real_inverse = cell_tables()
    consts = (
        jnp.asarray(to_strain, f32),
        jnp.asarray(to_force, f32),
        jnp.asarray(pick, bf16),
        jnp.asarray(coefs, f32),
        jnp.asarray(first, bf16),
        jnp.asarray(forward, bf16),
        jnp.asarray(inverse, bf16),
        jnp.asarray(real_forward, bf16),
        jnp.asarray(real_inverse, bf16),
    )
    vmem = pl.BlockSpec(memory_space=pltpu.VMEM)
    rows = 6 * slots

    def body(*refs):
        kernel(layers, slots, *refs)

    return pl.pallas_call(
        body,
        out_shape=(
            jax.ShapeDtypeStruct((layers * 8, NODE_PAD), f32),
            jax.ShapeDtypeStruct(damage.shape, bf16),
        ),
        in_specs=[pl.BlockSpec(memory_space=pltpu.SMEM)] + [vmem] * 14,
        out_specs=(vmem, vmem),
        scratch_shapes=[
            pltpu.VMEM((6 * CELL, slots, PLANE), f32),
            pltpu.VMEM((7, rows, 2 * PLANE), bf16),
            pltpu.VMEM((2, rows, PLANE), bf16),
            pltpu.VMEM((7, rows, 2 * PLANE), f32),
            pltpu.VMEM((2, rows, PLANE), f32),
            pltpu.VMEM((rows, 2 * PLANE), f32),
            pltpu.VMEM((rows, 2 * PLANE), bf16),
            pltpu.VMEM((6, slots, HALF), f32),
            pltpu.VMEM((48, layers * EXY * EXY), f32),
            pltpu.VMEM((6, slots, HALF), f32),
        ],
        compiler_params=pltpu.CompilerParams(vmem_limit_bytes=44 * 1024 * 1024),
        cost_estimate=pl.CostEstimate(flops=10**10, bytes_accessed=8 * 10**6, transcendentals=0),
        interpret=interpret,
    )(count, nodes, modulus, points, damage, voxel, *consts)


def body(displacement, macro_modulus, damaged_count, damaged_points, damage, voxel_modulus):
    layers = displacement.shape[1]
    axes = ("dom", "sub")
    below = shifted(displacement[:, layers - 1 :], axes, 1)
    grid = jnp.concatenate([below, displacement], axis=1)
    nodes = jnp.stack([grid[:, :layers], grid[:, 1:]]).transpose(2, 0, 1, 3)
    nodes = nodes.reshape(layers, 6, NODES)
    nodes = jnp.pad(nodes, ((0, 0), (0, 2), (0, NODE_PAD - NODES))).reshape(layers * 8, NODE_PAD)
    force, new_damage = run_kernel(
        damaged_count,
        nodes,
        macro_modulus,
        damaged_points.reshape(-1, 1),
        damage,
        voxel_modulus,
        layers,
    )
    force = force.reshape(layers, 8, NODE_PAD)[:, :, :NODES]
    from_above = shifted(force[:1, 0:3], axes, -1)
    lower = jnp.concatenate([force[1:, 0:3], from_above], axis=0)
    own_forces = (force[:, 3:6] + lower).transpose(1, 0, 2)
    return (own_forces, new_damage)


def solution(mesh):
    return jax.shard_map(
        body,
        mesh=mesh,
        in_specs=(
            P(None, ("dom", "sub"), None),
            P(None, ("dom", "sub")),
            P(("dom", "sub")),
            P(("dom", "sub"), None),
            P(("dom", "sub"), None),
            P(("dom", "sub"), None),
        ),
        out_specs=(P(None, ("dom", "sub"), None), P(("dom", "sub"), None)),
        check_vma=False,
    )
```

profile of v0, /device:TPU:23, one launch (start us, length us, event | category | flops | bytes accessed | tf_op | source)
XLA Modules:
  0.0 46.8 jit_solution(17644846340873528256)
XLA Ops:
  0.6 0.0 copy-start.7
  0.6 0.8 %slice.19 = f32[3,1,289]{2,1,0:T(1,128)S(1)} slice(f32[3,4,289]{2,1,0:T(4,128)} %param.15), slice={[0:3], [3:4], [0:289]} | slice | bytes 6936 | tf_op jit(solution)/shard_map/slice | solution.py:524
  1.4 3.7 %collective-permute-start = (f32[3,1,289]{2,1,0:T(1,128)S(1)}, f32[3,1,289]{2,1,0:T(1,128)S(1)}, u32[]{:S(2)}, u32[]{:S(2)}) collective-permute-start(f32[3,1,289]{2,1,0:T(1,128)S(1)} %slice.19), channel_id=1, source_target_pairs={{0,1},{1,2},{2,3},{3,4},{4,5},{5,6},{6,7},{7,8},{8,9},{9,10},{10,1... | collective-permute-start | bytes 10412 | tf_op jit(solution)/shard_map/ppermute | solution.py:39
  5.7 0.7 %copy.18.refs_3_ = s32[64,1]{1,0:T(8,128)S(1)} copy(s32[64,1]{0,1:T(1,128)} %bitcast.17) | data formatting | bytes 512 | tf_op jit(solution)/shard_map/reshape | solution.py:533
  6.5 0.0 collective-permute-done
  6.5 0.7 %fusion = f32[1,3,4,289]{3,2,1,0:T(4,128)S(1)} fusion(f32[3,4,289]{2,1,0:T(4,128)} %param.15, f32[3,1,289]{2,1,0:T(1,128)S(1)} %collective-permute-done), kind=kLoop, calls=%fused_computation.3 | loop fusion | flops 3468 | bytes 31212 | tf_op jit(solution)/shard_map/stack | solution.py:526
  7.2 0.7 %pad_maximum_fusion = f32[2,3,4,289]{3,2,1,0:T(4,128)S(1)} fusion(f32[1,3,4,289]{3,2,1,0:T(4,128)} %bitcast.16, f32[1,3,4,289]{3,2,1,0:T(4,128)S(1)} %fusion), kind=kLoop, calls=%fused_computation.1 | loop fusion | flops 6936 | bytes 55488 | tf_op jit(solution)/shard_map/stack | solution.py:526
  8.0 0.0 copy-start.2
  8.0 0.0 copy-start.10
  8.0 0.0 copy-start.11
  8.0 0.0 copy-done.7
  8.0 0.7 %copy-done.2 = f32[8,1024]{1,0:T(8,128)S(1)} copy-done((f32[8,1024]{1,0:T(8,128)S(1)}, f32[8,1024]{1,0:T(8,128)}, u32[]{:S(2)}) %copy-start.2) | copy-done | bytes 32792
  8.7 1.0 %copy-done = bf16[64,4096]{1,0:T(8,128)(2,1)S(1)} copy-done((bf16[64,4096]{1,0:T(8,128)(2,1)S(1)}, bf16[64,4096]{1,0:T(8,128)(2,1)}, u32[]{:S(2)}) %copy-start) | copy-done | bytes 524312
  9.8 1.0 %copy-done.1 = bf16[64,4096]{1,0:T(8,128)(2,1)S(1)} copy-done((bf16[64,4096]{1,0:T(8,128)(2,1)S(1)}, bf16[64,4096]{1,0:T(8,128)(2,1)}, u32[]{:S(2)}) %copy-start.1) | copy-done | bytes 524312
  10.8 1.2 %copy-done.3 = bf16[9,32,1536]{2,1,0:T(8,128)(2,1)S(1)} copy-done((bf16[9,32,1536]{2,1,0:T(8,128)(2,1)S(1)}, bf16[9,32,1536]{2,1,0:T(8,128)(2,1)}, u32[]{:S(2)}) %copy-start.3) | copy-done | bytes 884760
  12.0 1.1 %copy-done.4 = bf16[384,1024]{1,0:T(8,128)(2,1)S(1)} copy-done((bf16[384,1024]{1,0:T(8,128)(2,1)S(1)}, bf16[384,1024]{1,0:T(8,128)(2,1)}, u32[]{:S(2)}) %copy-start.4) | copy-done | bytes 786456
  13.1 1.0 %copy-done.5 = bf16[512,512]{1,0:T(8,128)(2,1)S(1)} copy-done((bf16[512,512]{1,0:T(8,128)(2,1)S(1)}, bf16[512,512]{1,0:T(8,128)(2,1)}, u32[]{:S(2)}) %copy-start.5) | copy-done | bytes 524312
  14.2 1.0 %copy-done.6 = bf16[512,512]{1,0:T(8,128)(2,1)S(1)} copy-done((bf16[512,512]{1,0:T(8,128)(2,1)S(1)}, bf16[512,512]{1,0:T(8,128)(2,1)}, u32[]{:S(2)}) %copy-start.6) | copy-done | bytes 524312
  15.2 0.9 %copy-done.8 = bf16[256,256]{1,0:T(8,128)(2,1)S(1)} copy-done((bf16[256,256]{1,0:T(8,128)(2,1)S(1)}, bf16[256,256]{1,0:T(8,128)(2,1)}, u32[]{:S(2)}) %copy-start.8) | copy-done | bytes 131096
  16.1 0.9 %copy-done.9 = bf16[256,256]{1,0:T(8,128)(2,1)S(1)} copy-done((bf16[256,256]{1,0:T(8,128)(2,1)S(1)}, bf16[256,256]{1,0:T(8,128)(2,1)}, u32[]{:S(2)}) %copy-start.9) | copy-done | bytes 131096
  17.0 22.4 %shard_map.158 = (f32[32,384]{1,0:T(8,128)S(1)}, bf16[64,4096]{1,0:T(8,128)(2,1)}) custom-call(s32[1]{0:T(128)S(6)} %copy.26.refs_0_, f32[32,384]{1,0:T(8,128)S(1)} %pad_bitcast_fusion.refs_1_, f32[8,1024]{1,0:T(8,128)S(1)} %copy-done.2, s32[64,1]{1,0:T(8,128)S(1)} %copy.18.refs_3_, bf16[64,4096]{1,0:T(8,128)(2,1)S(1)} %copy-done, ...), custom_call_target="tpu_custom_call" | custom-call | flops 10000000000 | bytes 8000000 | tf_op jit(solution)/shard_map/pallas_call | solution.py:495
  39.5 2.4 %collective-permute-start.1 = (f32[1,3,289]{2,0,1:T(1,128)S(1)}, f32[1,3,289]{2,0,1:T(1,128)S(1)}, u32[]{:S(2)}, u32[]{:S(2)}) collective-permute-start(f32[1,3,289]{2,0,1:T(1,128)S(1)} %copy.24), channel_id=1, source_target_pairs={{1,0},{2,1},{3,2},{4,3},{5,4},{6,5},{7,6},{8,7},{9,8},{10,9},{11,1... | collective-permute-start | bytes 10412 | tf_op jit(solution)/shard_map/ppermute | solution.py:39
  41.9 4.3 %collective-permute-done.1 = f32[1,3,289]{2,0,1:T(1,128)S(1)} collective-permute-done((f32[1,3,289]{2,0,1:T(1,128)S(1)}, f32[1,3,289]{2,0,1:T(1,128)S(1)}, u32[]{:S(2)}, u32[]{:S(2)}) %collective-permute-start.1) | collective-permute-done | bytes 3500 | tf_op jit(solution)/shard_map/ppermute | solution.py:39
  46.2 0.6 %fusion.1 = f32[3,4,289]{2,1,0:T(4,128)} fusion(f32[1,3,289]{2,0,1:T(1,128)S(1)} %collective-permute-done.1, f32[3,3,289]{2,0,1:T(4,128)S(1)} %copy.23, f32[4,3,289]{2,1,0:T(4,128)S(1)} %slice.24), kind=kLoop, calls=%fused_computation.5 | loop fusion | flops 6936 | bytes 41616 | tf_op jit(solution)/shard_map/transpose | solution.py:541
  (17 shorter events, 0.1 us)
Async XLA Ops:
  0.6 7.4 %copy-start.7 = (f32[9,24,256]{2,1,0:T(8,128)S(1)}, f32[9,24,256]{2,1,0:T(8,128)}, u32[]{:S(2)}) copy-start(f32[9,24,256]{2,1,0:T(8,128)} %constant.24.clone.refs_9_) | copy-start | bytes 663556
  1.4 5.1 %collective-permute-start = (f32[3,1,289]{2,1,0:T(1,128)S(1)}, f32[3,1,289]{2,1,0:T(1,128)S(1)}, u32[]{:S(2)}, u32[]{:S(2)}) collective-permute-start(f32[3,1,289]{2,1,0:T(1,128)S(1)} %slice.19), channel_id=1, source_target_pairs={{0,1},{1,2},{2,3},{3,4},{4,5},{5,6},{6,7},{7,8},{8,9},{9,10},{10,1... | collective-permute-start | bytes 10412 | tf_op jit(solution)/shard_map/ppermute | solution.py:39
  8.0 0.8 %copy-start.2 = (f32[8,1024]{1,0:T(8,128)S(1)}, f32[8,1024]{1,0:T(8,128)}, u32[]{:S(2)}) copy-start(f32[8,1024]{1,0:T(8,128)} %refs_2_.1) | copy-start | bytes 98308
  8.0 0.8 %copy-start.10 = (f32[48,32]{1,0:T(8,128)S(1)}, f32[48,32]{1,0:T(8,128)}, u32[]{:S(2)}) copy-start(f32[48,32]{1,0:T(8,128)} %constant.21.clone.refs_6_) | copy-start | bytes 18436
  8.0 0.7 %copy-start.11 = (f32[32,48]{1,0:T(8,128)S(1)}, f32[32,48]{1,0:T(8,128)}, u32[]{:S(2)}) copy-start(f32[32,48]{1,0:T(8,128)} %constant.22.clone.refs_7_) | copy-start | bytes 18436
  8.7 1.0 %copy-start = (bf16[64,4096]{1,0:T(8,128)(2,1)S(1)}, bf16[64,4096]{1,0:T(8,128)(2,1)}, u32[]{:S(2)}) copy-start(bf16[64,4096]{1,0:T(8,128)(2,1)} %refs_4_.1) | copy-start | bytes 1572868
  9.8 1.0 %copy-start.1 = (bf16[64,4096]{1,0:T(8,128)(2,1)S(1)}, bf16[64,4096]{1,0:T(8,128)(2,1)}, u32[]{:S(2)}) copy-start(bf16[64,4096]{1,0:T(8,128)(2,1)} %refs_5_.1) | copy-start | bytes 1572868
  10.8 1.2 %copy-start.3 = (bf16[9,32,1536]{2,1,0:T(8,128)(2,1)S(1)}, bf16[9,32,1536]{2,1,0:T(8,128)(2,1)}, u32[]{:S(2)}) copy-start(bf16[9,32,1536]{2,1,0:T(8,128)(2,1)} %constant.25.clone.refs_10_) | copy-start | bytes 2654212
  12.0 1.1 %copy-start.4 = (bf16[384,1024]{1,0:T(8,128)(2,1)S(1)}, bf16[384,1024]{1,0:T(8,128)(2,1)}, u32[]{:S(2)}) copy-start(bf16[384,1024]{1,0:T(8,128)(2,1)} %constant.23.clone.refs_8_) | copy-start | bytes 2359300
  13.1 1.0 %copy-start.5 = (bf16[512,512]{1,0:T(8,128)(2,1)S(1)}, bf16[512,512]{1,0:T(8,128)(2,1)}, u32[]{:S(2)}) copy-start(bf16[512,512]{1,0:T(8,128)(2,1)} %constant.27.clone.refs_12_) | copy-start | bytes 1572868
  14.2 1.0 %copy-start.6 = (bf16[512,512]{1,0:T(8,128)(2,1)S(1)}, bf16[512,512]{1,0:T(8,128)(2,1)}, u32[]{:S(2)}) copy-start(bf16[512,512]{1,0:T(8,128)(2,1)} %constant.26.clone.refs_11_) | copy-start | bytes 1572868
  15.2 0.9 %copy-start.8 = (bf16[256,256]{1,0:T(8,128)(2,1)S(1)}, bf16[256,256]{1,0:T(8,128)(2,1)}, u32[]{:S(2)}) copy-start(bf16[256,256]{1,0:T(8,128)(2,1)} %constant.29.clone.refs_14_) | copy-start | bytes 393220
  16.1 0.9 %copy-start.9 = (bf16[256,256]{1,0:T(8,128)(2,1)S(1)}, bf16[256,256]{1,0:T(8,128)(2,1)}, u32[]{:S(2)}) copy-start(bf16[256,256]{1,0:T(8,128)(2,1)} %constant.28.clone.refs_13_) | copy-start | bytes 393220
  39.5 6.7 %collective-permute-start.1 = (f32[1,3,289]{2,0,1:T(1,128)S(1)}, f32[1,3,289]{2,0,1:T(1,128)S(1)}, u32[]{:S(2)}, u32[]{:S(2)}) collective-permute-start(f32[1,3,289]{2,0,1:T(1,128)S(1)} %copy.24), channel_id=1, source_target_pairs={{1,0},{2,1},{3,2},{4,3},{5,4},{6,5},{7,6},{8,7},{9,8},{10,9},{11,1... | collective-permute-start | bytes 10412 | tf_op jit(solution)/shard_map/ppermute | solution.py:39
where the time goes:
time: 47.5 us; the launch traced here: 46.8 us
  Pallas kernels  22.4 us (47%)
  local copies, waits for them, and re-layouts  10.6 us (22%)
  starting transfers between devices  6.07 us (13%)
  waiting for transfers between devices  4.28 us (9%)
  other arithmetic  2.09 us (4%)
  between operations  1.39 us (3%)
    pallas_call x1, Pallas kernels, run_kernel(): pl.pallas_call(body, out_shape=(jax.ShapeDtypeStruct((layers * 8, NODE_PA...  22.4 us
    unnamed x26, local copies, waits for them, and re-layouts  9.01 us
    ppermute x2, starting transfers between devices, shifted(): lax.ppermute(value, axis, [(source, source + steps) for source in range(i...  6.07 us
    ppermute x2, waiting for transfers between devices, shifted(): lax.ppermute(value, axis, [(source, source + steps) for source in range(i...  4.28 us
    another operation x2, other arithmetic, body(): nodes = jnp.stack([grid[:, :layers], grid[:, 1:]]).transpose(2, 0, 1, 3)  1.47 us
  transfers between devices with their start and end apart: 2, of which 1 were waited for; matrix products, arithmetic and copies ran while one was open for 2% of the time, Pallas kernels for 0%

commit v1 on v0

--- a/solution.py
+++ b/solution.py
@@ -1,3 +1,4 @@
+import functools
 import math
 
 import jax
@@ -30,13 +31,8 @@
         )
 C1, C2, C3 = (math.cos(math.pi * n / 8) for n in (1, 2, 3))
 f32, bf16 = jnp.float32, jnp.bfloat16
+MESH = pl.DeviceIdType.MESH
 HIGHEST = lax.Precision.HIGHEST
-
-
-def shifted(value, axis, steps):
-    count = lax.axis_size(axis)
-    initial, last = (max(0, -steps), min(count, count - steps))
-    return lax.ppermute(value, axis, [(source, source + steps) for source in range(initial, last)])
 
 
 def shape_table():
@@ -226,21 +222,21 @@
     slots,
     count_ref,
     nodes_ref,
-    modulus_ref,
     points_ref,
-    damage_ref,
-    voxel_ref,
-    strain_tab,
-    force_tab,
-    pick_tab,
-    coef_tab,
-    first_tab,
-    forward_tab,
-    inverse_tab,
-    real_forward,
-    real_inverse,
+    modulus_hbm,
+    pick_hbm,
+    strain_hbm,
+    damage_hbm,
+    voxel_hbm,
+    forward_hbm,
+    first_hbm,
+    inverse_hbm,
+    real_forward_hbm,
+    real_inverse_hbm,
+    coef_hbm,
+    force_hbm,
     force_ref,
-    new_ref,
+    new_hbm,
     field,
     spec_c,
     spec_r,
@@ -251,7 +247,58 @@
     macro,
     stress_s,
     acc,
+    new_ref,
+    modulus_ref,
+    pick_tab,
+    strain_tab,
+    damage_ref,
+    voxel_ref,
+    forward_tab,
+    first_tab,
+    inverse_tab,
+    real_forward,
+    real_inverse,
+    coef_tab,
+    force_tab,
+    in_sems,
+    out_sems,
 ):
+    sources = (
+        modulus_hbm,
+        pick_hbm,
+        strain_hbm,
+        damage_hbm,
+        voxel_hbm,
+        forward_hbm,
+        first_hbm,
+        inverse_hbm,
+        real_forward_hbm,
+        real_inverse_hbm,
+        coef_hbm,
+        force_hbm,
+    )
+    targets = (
+        modulus_ref,
+        pick_tab,
+        strain_tab,
+        damage_ref,
+        voxel_ref,
+        forward_tab,
+        first_tab,
+        inverse_tab,
+        real_forward,
+        real_inverse,
+        coef_tab,
+        force_tab,
+    )
+    loads = [
+        pltpu.make_async_copy(source, target, in_sems.at[n])
+        for n, (source, target) in enumerate(zip(sources, targets))
+    ]
+    for load in loads:
+        load.start()
+    for load in loads[:3]:
+        load.wait()
     elems = layers * EXY * EXY
     chunks = slots // ROWS
     count = count_ref[0]
@@ -274,7 +321,13 @@
     stress = jnp.concatenate([modulus * law[k] for k in range(6)], axis=0)
     stress_s[...] = stress
 
-    points = points_ref[...]
+    square = (slots, slots)
+    diagonal = lax.broadcasted_iota(jnp.int32, square, 0) == lax.broadcasted_iota(
+        jnp.int32, square, 1
+    )
+    spread_points = jnp.broadcast_to(points_ref[...].astype(f32), square)
+    points = jnp.sum(jnp.where(diagonal, spread_points, 0.0), axis=1, keepdims=True)
+    points = points.astype(jnp.int32)
     element = points % elems
     gauss = points // elems
     hot = (lax.broadcasted_iota(jnp.int32, (slots, elems), 1) == element).astype(f32).astype(bf16)
@@ -299,6 +352,8 @@
         upper = jnp.where((lane32 == k) | (lane32 == 12 + k), high, upper)
         upper = jnp.where(lane32 == 6 + k, mean_law[k] - high, upper)
     mean_parts = upper.astype(bf16)
+    for load in loads[3:5]:
+        load.wait()
     for r in range(chunks):
         rows = slice(r * ROWS, (r + 1) * ROWS)
         for h in range(2):
@@ -351,6 +406,8 @@
                     field[k * CELL + x, r * ROWS : (r + 1) * ROWS, lanes] = base - values[x]
         return carry
 
+    for load in loads[5:]:
+        load.wait()
     lax.fori_loop(0, 7, first_c, 0)
     lax.fori_loop(0, 2, first_r, 0)
     lax.fori_loop(0, 6, to_strain, 0)
@@ -423,6 +480,7 @@
     lax.fori_loop(0, 2, second_r, 0)
     lax.fori_loop(0, 6, to_strain, 0)
 
+    stores = []
     for r in range(chunks):
         rows = slice(r * ROWS, (r + 1) * ROWS)
         live = lax.broadcasted_iota(jnp.int32, (ROWS, PLANE), 0) + r * ROWS < count
@@ -444,6 +502,8 @@
         sums = lax.fori_loop(0, CELL, finish, (jnp.zeros((ROWS, HALF), f32),) * 6)
         for k in range(6):
             acc[k, rows] = sums[k]
+        stores.append(pltpu.make_async_copy(new_ref.at[rows], new_hbm.at[rows], out_sems.at[r]))
+        stores[r].start()
 
     alive = lax.broadcasted_iota(jnp.int32, (slots, 1), 0) < count
     lane128 = lax.broadcasted_iota(jnp.int32, (slots, HALF), 1)
@@ -469,24 +529,29 @@
             parts3(by_layer), pick_tab[...], (((1,), (1,)), ((), ())), preferred_element_type=f32
         )
     )
+    for store in stores:
+        store.wait()
 
 
 def run_kernel(count, nodes, modulus, points, damage, voxel, layers, interpret=False):
     slots = damage.shape[0]
     to_strain, to_force, pick = macro_tables()
     coefs, first, forward, inverse, real_forward, real_inverse = cell_tables()
-    consts = (
+    operands = (
+        modulus,
+        jnp.asarray(pick, bf16),
         jnp.asarray(to_strain, f32),
-        jnp.asarray(to_force, f32),
-        jnp.asarray(pick, bf16),
-        jnp.asarray(coefs, f32),
+        damage,
+        voxel,
+        jnp.asarray(forward, bf16),
         jnp.asarray(first, bf16),
-        jnp.asarray(forward, bf16),
         jnp.asarray(inverse, bf16),
         jnp.asarray(real_forward, bf16),
         jnp.asarray(real_inverse, bf16),
-    )
-    vmem = pl.BlockSpec(memory_space=pltpu.VMEM)
+        jnp.asarray(coefs, f32),
+        jnp.asarray(to_force, f32),
+    )
+    vmem, anywhere = pl.BlockSpec(memory_space=pltpu.VMEM), pl.BlockSpec(memory_space=pl.ANY)
     rows = 6 * slots
 
     def body(*refs):
@@ -498,8 +563,8 @@
             jax.ShapeDtypeStruct((layers * 8, NODE_PAD), f32),
             jax.ShapeDtypeStruct(damage.shape, bf16),
         ),
-        in_specs=[pl.BlockSpec(memory_space=pltpu.SMEM)] + [vmem] * 14,
-        out_specs=(vmem, vmem),
+        in_specs=[pl.BlockSpec(memory_space=pltpu.SMEM), vmem, vmem] + [anywhere] * 12,
+        out_specs=(vmem, anywhere),
         scratch_shapes=[
             pltpu.VMEM((6 * CELL, slots, PLANE), f32),
             pltpu.VMEM((7, rows, 2 * PLANE), bf16),
@@ -511,34 +576,141 @@
             pltpu.VMEM((6, slots, HALF), f32),
             pltpu.VMEM((48, layers * EXY * EXY), f32),
             pltpu.VMEM((6, slots, HALF), f32),
+            pltpu.VMEM(damage.shape, bf16),
+        ]
+        + [pltpu.VMEM(operand.shape, operand.dtype) for operand in operands]
+        + [
+            pltpu.SemaphoreType.DMA((len(operands),)),
+            pltpu.SemaphoreType.DMA((slots // ROWS,)),
         ],
         compiler_params=pltpu.CompilerParams(vmem_limit_bytes=44 * 1024 * 1024),
         cost_estimate=pl.CostEstimate(flops=10**10, bytes_accessed=8 * 10**6, transcendentals=0),
         interpret=interpret,
-    )(count, nodes, modulus, points, damage, voxel, *consts)
+    )(count, nodes, points, *operands)
+
+
+def neighbour(steps, across):
+    place = lax.axis_index("dom") * across + lax.axis_index("sub") + steps
+    return (place // across, place % across)
+
+
+def spread_kernel(layers, total, across, moved_ref, nodes_ref, sent, landed, send_sem, recv_sem):
+    place = lax.axis_index("dom") * across + lax.axis_index("sub")
+    barrier = pltpu.get_barrier_semaphore()
+
+    @pl.when(place > 0)
+    def _():
+        pl.semaphore_signal(
+            barrier, inc=1, device_id=neighbour(-1, across), device_id_type=MESH
+        )
+
+    sent[...] = jnp.zeros_like(sent)
+    for i in range(3):
+        sent[i : i + 1, 0:NODES] = moved_ref[i, layers - 1 : layers, :]
+    copy = pltpu.make_async_remote_copy(
+        src_ref=sent,
+        dst_ref=landed,
+        send_sem=send_sem,
+        recv_sem=recv_sem,
+        device_id=neighbour(1, across),
+        device_id_type=MESH,
+    )
+
+    @pl.when(place < total - 1)
+    def _():
+        pl.semaphore_wait(barrier, 1)
+        copy.start()
+
+    nodes_ref[...] = jnp.zeros_like(nodes_ref)
+    for z in range(layers):
+        for cz in range(2):
+            for i in range(3):
+                if z + cz > 0:
+                    row = z * 8 + cz * 3 + i
+                    nodes_ref[row : row + 1, 0:NODES] = moved_ref[i, z + cz - 1 : z + cz, :]
+
+    @pl.when(place > 0)
+    def _():
+        copy.wait_recv()
+        nodes_ref[0:3, :] = landed[0:3, :]
+
+    @pl.when(place < total - 1)
+    def _():
+        copy.wait_send()
+
+
+def gather_kernel(layers, total, across, force_ref, out_ref, landed, send_sem, recv_sem):
+    place = lax.axis_index("dom") * across + lax.axis_index("sub")
+    barrier = pltpu.get_barrier_semaphore()
+
+    @pl.when(place < total - 1)
+    def _():
+        pl.semaphore_signal(
+            barrier, inc=1, device_id=neighbour(1, across), device_id_type=MESH
+        )
+
+    copy = pltpu.make_async_remote_copy(
+        src_ref=force_ref.at[0:8],
+        dst_ref=landed,
+        send_sem=send_sem,
+        recv_sem=recv_sem,
+        device_id=neighbour(-1, across),
+        device_id_type=MESH,
+    )
+
+    @pl.when(place > 0)
+    def _():
+        pl.semaphore_wait(barrier, 1)
+        copy.start()
+
+    for z in range(layers):
+        for i in range(3):
+            value = force_ref[z * 8 + 3 + i : z * 8 + 4 + i, 0:NODES]
+            if z + 1 < layers:
+                value = value + force_ref[z * 8 + 8 + i : z * 8 + 9 + i, 0:NODES]
+            out_ref[i, z : z + 1, :] = value
+
+    @pl.when(place < total - 1)
+    def _():
+        copy.wait_recv()
+        for i in range(3):
+            out_ref[i, layers - 1 : layers, :] += landed[i : i + 1, 0:NODES]
+
+    @pl.when(place > 0)
+    def _():
+        copy.wait_send()
+
+
+def exchange(function, value, shape, scratch, collective_id):
+    vmem = pl.BlockSpec(memory_space=pltpu.VMEM)
+    tile = pltpu.VMEM((8, NODE_PAD), f32)
+    return pl.pallas_call(
+        function,
+        out_shape=jax.ShapeDtypeStruct(shape, f32),
+        in_specs=[vmem],
+        out_specs=vmem,
+        scratch_shapes=[tile] * scratch + [pltpu.SemaphoreType.DMA] * 2,
+        compiler_params=pltpu.CompilerParams(collective_id=collective_id, has_side_effects=True),
+    )(value)
 
 
 def body(displacement, macro_modulus, damaged_count, damaged_points, damage, voxel_modulus):
     layers = displacement.shape[1]
-    axes = ("dom", "sub")
-    below = shifted(displacement[:, layers - 1 :], axes, 1)
-    grid = jnp.concatenate([below, displacement], axis=1)
-    nodes = jnp.stack([grid[:, :layers], grid[:, 1:]]).transpose(2, 0, 1, 3)
-    nodes = nodes.reshape(layers, 6, NODES)
-    nodes = jnp.pad(nodes, ((0, 0), (0, 2), (0, NODE_PAD - NODES))).reshape(layers * 8, NODE_PAD)
+    across = lax.axis_size("sub")
+    total = lax.axis_size("dom") * across
+    nodes = exchange(
+        functools.partial(spread_kernel, layers, total, across),
+        displacement,
+        (layers * 8, NODE_PAD),
+        2,
+        0,
+    )
     force, new_damage = run_kernel(
-        damaged_count,
-        nodes,
-        macro_modulus,
-        damaged_points.reshape(-1, 1),
-        damage,
-        voxel_modulus,
-        layers,
-    )
-    force = force.reshape(layers, 8, NODE_PAD)[:, :, :NODES]
-    from_above = shifted(force[:1, 0:3], axes, -1)
-    lower = jnp.concatenate([force[1:, 0:3], from_above], axis=0)
-    own_forces = (force[:, 3:6] + lower).transpose(1, 0, 2)
+        damaged_count, nodes, macro_modulus, damaged_points, damage, voxel_modulus, layers
+    )
+    own_forces = exchange(
+        functools.partial(gather_kernel, layers, total, across), force, displacement.shape, 1, 1
+    )
     return (own_forces, new_damage)
 
 

time: 47.5 us -> 47.9 us (level)
  Pallas kernels: 22.4 us -> 33.8 us
  starting transfers between devices: 6.07 us -> 0 us
  waiting for transfers between devices: 4.28 us -> 0 us
  other arithmetic: 2.09 us -> 0 us
  local copies, waits for them, and re-layouts: 10.6 us -> 12 us
    pallas_call x0 -> x2, Pallas kernels: none -> 10.9 us  [exchange(): pl.pallas_call(function, out_shape=jax.ShapeDtypeStruct(shape, f32), in_s...]
    ppermute x2 -> x0, starting transfers between devices: 6.07 us -> none  [shifted(): lax.ppermute(value, axis, [(source, source + steps) for source in range(i...]
    ppermute x2 -> x0, waiting for transfers between devices: 4.28 us -> none  [shifted(): lax.ppermute(value, axis, [(source, source + steps) for source in range(i...]
    unnamed x26 -> x31, local copies, waits for them, and re-layouts: 9.01 us -> 12 us
    another operation x2 -> x0, other arithmetic: 1.47 us -> none  [body(): nodes = jnp.stack([grid[:, :layers], grid[:, 1:]]).transpose(2, 0, 1, 3)]
    slice x4 -> x0, local copies, waits for them, and re-layouts: 0.79 us -> none  [the longest x1 0.77 us: body(): below = shifted(displacement[:, layers - 1:], axes, 1)]
    reshape x3 -> x0, local copies, waits for them, and re-layouts: 0.76 us -> none  [the longest x1 0.75 us: body(): damaged_points.reshape(-1, 1)]
    transpose x1 -> x0, other arithmetic: 0.62 us -> none  [body(): own_forces = (force[:, 3:6] + lower).transpose(1, 0, 2)]
  transfers between devices with their start and end apart: 2 -> 0, of which waited for: 1 -> 0; matrix products, arithmetic and copies ran while one was open for 2% -> 0% of each run, Pallas kernels for 0% -> 0%
where the time goes in v1:
time: 47.9 us; the launch traced here: 47.2 us
  Pallas kernels  33.8 us (71%)
  local copies, waits for them, and re-layouts  12 us (25%)
  between operations  1.4 us (3%)
    pallas_call x1, Pallas kernels, run_kernel(): pl.pallas_call(body, out_shape=(jax.ShapeDtypeStruct((layers * 8, NODE_PA...  23 us
    unnamed x31, local copies, waits for them, and re-layouts  12 us
    pallas_call x2, Pallas kernels, exchange(): pl.pallas_call(function, out_shape=jax.ShapeDtypeStruct(shape, f32), in_s...  10.9 us

profile of v1, /device:TPU:23, one launch (start us, length us, event | category | flops | bytes accessed | tf_op | source)
XLA Modules:
  0.0 47.2 jit_solution(6337717355186438139)
XLA Ops:
  0.6 0.0 copy-start.14
  1.3 0.0 copy-start.4
  1.3 0.0 copy-start.13
  1.3 4.0 %shard_map.158.refs_1_ = f32[32,384]{1,0:T(8,128)} custom-call(f32[3,4,289]{2,1,0:T(4,128)} %moved_ref.1), custom_call_target="tpu_custom_call" | custom-call | tf_op jit(solution)/shard_map/pallas_call | solution.py:687
  5.3 0.0 copy-done.14
  5.3 0.0 copy-done.4
  5.3 0.0 copy-done.5
  5.3 0.0 copy-done.13
  5.4 0.0 copy-start.1
  5.4 0.8 %copy-done.1 = f32[32,384]{1,0:T(8,128)S(1)} copy-done((f32[32,384]{1,0:T(8,128)S(1)}, f32[32,384]{1,0:T(8,128)}, u32[]{:S(2)}) %copy-start.1) | copy-done | bytes 49176
  6.2 1.0 %copy-done.2 = bf16[64,4096]{1,0:T(8,128)(2,1)S(1)} copy-done((bf16[64,4096]{1,0:T(8,128)(2,1)S(1)}, bf16[64,4096]{1,0:T(8,128)(2,1)}, u32[]{:S(2)}) %copy-start.2) | copy-done | bytes 524312
  7.2 1.0 %copy-done.3 = bf16[64,4096]{1,0:T(8,128)(2,1)S(1)} copy-done((bf16[64,4096]{1,0:T(8,128)(2,1)S(1)}, bf16[64,4096]{1,0:T(8,128)(2,1)}, u32[]{:S(2)}) %copy-start.3) | copy-done | bytes 524312
  8.2 1.2 %copy-done.6 = bf16[9,32,1536]{2,1,0:T(8,128)(2,1)S(1)} copy-done((bf16[9,32,1536]{2,1,0:T(8,128)(2,1)S(1)}, bf16[9,32,1536]{2,1,0:T(8,128)(2,1)}, u32[]{:S(2)}) %copy-start.6) | copy-done | bytes 884760
  9.4 1.1 %copy-done.7 = bf16[384,1024]{1,0:T(8,128)(2,1)S(1)} copy-done((bf16[384,1024]{1,0:T(8,128)(2,1)S(1)}, bf16[384,1024]{1,0:T(8,128)(2,1)}, u32[]{:S(2)}) %copy-start.7) | copy-done | bytes 786456
  10.5 1.0 %copy-done.8 = bf16[512,512]{1,0:T(8,128)(2,1)S(1)} copy-done((bf16[512,512]{1,0:T(8,128)(2,1)S(1)}, bf16[512,512]{1,0:T(8,128)(2,1)}, u32[]{:S(2)}) %copy-start.8) | copy-done | bytes 524312
  11.6 1.0 %copy-done.9 = bf16[512,512]{1,0:T(8,128)(2,1)S(1)} copy-done((bf16[512,512]{1,0:T(8,128)(2,1)S(1)}, bf16[512,512]{1,0:T(8,128)(2,1)}, u32[]{:S(2)}) %copy-start.9) | copy-done | bytes 524312
  12.6 0.9 %copy-done.10 = f32[9,24,256]{2,1,0:T(8,128)S(1)} copy-done((f32[9,24,256]{2,1,0:T(8,128)S(1)}, f32[9,24,256]{2,1,0:T(8,128)}, u32[]{:S(2)}) %copy-start.10) | copy-done | bytes 221208
  13.6 0.9 %copy-done.11 = bf16[256,256]{1,0:T(8,128)(2,1)S(1)} copy-done((bf16[256,256]{1,0:T(8,128)(2,1)S(1)}, bf16[256,256]{1,0:T(8,128)(2,1)}, u32[]{:S(2)}) %copy-start.11) | copy-done | bytes 131096
  14.5 0.9 %copy-done.12 = bf16[256,256]{1,0:T(8,128)(2,1)S(1)} copy-done((bf16[256,256]{1,0:T(8,128)(2,1)S(1)}, bf16[256,256]{1,0:T(8,128)(2,1)}, u32[]{:S(2)}) %copy-start.12) | copy-done | bytes 131096
  15.4 23.0 %shard_map.159 = (f32[32,384]{1,0:T(8,128)S(1)}, bf16[64,4096]{1,0:T(8,128)(2,1)}) custom-call(s32[1]{0:T(128)S(6)} %copy.18.refs_0_, f32[32,384]{1,0:T(8,128)S(1)} %copy-done.1, s32[1,64]{1,0:T(1,128)S(1)} %copy-done.5, f32[8,1024]{1,0:T(8,128)S(1)} %copy-done.4, bf16[384,1024]{1,0:T(8,128)(2,1)S(1)} %copy-done.7, f32[48,32]{1,0:T(8,128)S(1)} %copy-done.13, ...), custom_call_target="tpu_custom_call" | custom-call | flops 10000000000 | bytes 8000000 | tf_op jit(solution)/shard_map/pallas_call | solution.py:560
  38.3 0.0 copy-start
  38.3 0.6 %copy-done = f32[32,384]{1,0:T(8,128)} copy-done((f32[32,384]{1,0:T(8,128)}, f32[32,384]{1,0:T(8,128)S(1)}, u32[]{:S(2)}) %copy-start) | copy-done | bytes 49176
  39.0 6.9 %shard_map.160 = f32[3,4,289]{2,1,0:T(4,128)} custom-call(f32[32,384]{1,0:T(8,128)} %copy-done), custom_call_target="tpu_custom_call" | custom-call | tf_op jit(solution)/shard_map/pallas_call | solution.py:687
  45.9 1.3 %copy.19 = f32[3,4,289]{2,1,0:T(4,128)} copy(f32[3,4,289]{2,1,0:T(4,128)} %shard_map.160) | data formatting | bytes 27744
  (10 shorter events, 0.0 us)
Async XLA Ops:
  0.6 4.7 %copy-start.14 = (f32[32,48]{1,0:T(8,128)S(1)}, f32[32,48]{1,0:T(8,128)}, u32[]{:S(2)}) copy-start(f32[32,48]{1,0:T(8,128)} %constant.26.clone.refs_14_) | copy-start | bytes 18436
  1.3 4.0 %copy-start.4 = (f32[8,1024]{1,0:T(8,128)S(1)}, f32[8,1024]{1,0:T(8,128)}, u32[]{:S(2)}) copy-start(f32[8,1024]{1,0:T(8,128)} %refs_3_.1) | copy-start | bytes 98308
  1.3 4.0 %copy-start.5 = (s32[1,64]{1,0:T(1,128)S(1)}, s32[1,64]{1,0:T(1,128)}, u32[]{:S(2)}) copy-start(s32[1,64]{1,0:T(1,128)} %refs_2_.1) | copy-start | bytes 772
  1.3 4.0 %copy-start.13 = (f32[48,32]{1,0:T(8,128)S(1)}, f32[48,32]{1,0:T(8,128)}, u32[]{:S(2)}) copy-start(f32[48,32]{1,0:T(8,128)} %constant.19.clone.refs_5_) | copy-start | bytes 18436
  5.4 0.8 %copy-start.1 = (f32[32,384]{1,0:T(8,128)S(1)}, f32[32,384]{1,0:T(8,128)}, u32[]{:S(2)}) copy-start(f32[32,384]{1,0:T(8,128)} %shard_map.158.refs_1_) | copy-start | bytes 147460
  6.2 1.0 %copy-start.2 = (bf16[64,4096]{1,0:T(8,128)(2,1)S(1)}, bf16[64,4096]{1,0:T(8,128)(2,1)}, u32[]{:S(2)}) copy-start(bf16[64,4096]{1,0:T(8,128)(2,1)} %refs_6_.1) | copy-start | bytes 1572868
  7.2 1.0 %copy-start.3 = (bf16[64,4096]{1,0:T(8,128)(2,1)S(1)}, bf16[64,4096]{1,0:T(8,128)(2,1)}, u32[]{:S(2)}) copy-start(bf16[64,4096]{1,0:T(8,128)(2,1)} %refs_7_.1) | copy-start | bytes 1572868
  8.2 1.2 %copy-start.6 = (bf16[9,32,1536]{2,1,0:T(8,128)(2,1)S(1)}, bf16[9,32,1536]{2,1,0:T(8,128)(2,1)}, u32[]{:S(2)}) copy-start(bf16[9,32,1536]{2,1,0:T(8,128)(2,1)} %constant.21.clone.refs_9_) | copy-start | bytes 2654212
  9.4 1.1 %copy-start.7 = (bf16[384,1024]{1,0:T(8,128)(2,1)S(1)}, bf16[384,1024]{1,0:T(8,128)(2,1)}, u32[]{:S(2)}) copy-start(bf16[384,1024]{1,0:T(8,128)(2,1)} %constant.18.clone.refs_4_) | copy-start | bytes 2359300
  10.5 1.0 %copy-start.8 = (bf16[512,512]{1,0:T(8,128)(2,1)S(1)}, bf16[512,512]{1,0:T(8,128)(2,1)}, u32[]{:S(2)}) copy-start(bf16[512,512]{1,0:T(8,128)(2,1)} %constant.22.clone.refs_10_) | copy-start | bytes 1572868
  11.6 1.0 %copy-start.9 = (bf16[512,512]{1,0:T(8,128)(2,1)S(1)}, bf16[512,512]{1,0:T(8,128)(2,1)}, u32[]{:S(2)}) copy-start(bf16[512,512]{1,0:T(8,128)(2,1)} %constant.20.clone.refs_8_) | copy-start | bytes 1572868
  12.6 0.9 %copy-start.10 = (f32[9,24,256]{2,1,0:T(8,128)S(1)}, f32[9,24,256]{2,1,0:T(8,128)}, u32[]{:S(2)}) copy-start(f32[9,24,256]{2,1,0:T(8,128)} %constant.25.clone.refs_13_) | copy-start | bytes 663556
  13.6 0.9 %copy-start.11 = (bf16[256,256]{1,0:T(8,128)(2,1)S(1)}, bf16[256,256]{1,0:T(8,128)(2,1)}, u32[]{:S(2)}) copy-start(bf16[256,256]{1,0:T(8,128)(2,1)} %constant.24.clone.refs_12_) | copy-start | bytes 393220
  14.5 0.9 %copy-start.12 = (bf16[256,256]{1,0:T(8,128)(2,1)S(1)}, bf16[256,256]{1,0:T(8,128)(2,1)}, u32[]{:S(2)}) copy-start(bf16[256,256]{1,0:T(8,128)(2,1)} %constant.23.clone.refs_11_) | copy-start | bytes 393220
  38.3 0.6 %copy-start = (f32[32,384]{1,0:T(8,128)}, f32[32,384]{1,0:T(8,128)S(1)}, u32[]{:S(2)}) copy-start(f32[32,384]{1,0:T(8,128)S(1)} %get-tuple-element.4.force_ref) | copy-start | bytes 147460

commit v2 on v1

--- a/solution.py
+++ b/solution.py
@@ -217,12 +217,19 @@
     ]
 
 
+def neighbour(steps, across):
+    place = lax.axis_index("dom") * across + lax.axis_index("sub") + steps
+    return (place // across, place % across)
+
+
 def kernel(
     layers,
     slots,
+    total,
+    across,
     count_ref,
-    nodes_ref,
-    points_ref,
+    moved_hbm,
+    points_hbm,
     modulus_hbm,
     pick_hbm,
     strain_hbm,
@@ -248,6 +255,13 @@
     stress_s,
     acc,
     new_ref,
+    nodes_ref,
+    forces,
+    sent,
+    landed_up,
+    landed_down,
+    moved_ref,
+    points_ref,
     modulus_ref,
     pick_tab,
     strain_tab,
@@ -262,8 +276,24 @@
     force_tab,
     in_sems,
     out_sems,
+    send_sems,
+    recv_sems,
 ):
+    place = lax.axis_index("dom") * across + lax.axis_index("sub")
+    barrier = pltpu.get_barrier_semaphore()
+    has_below, has_above = place > 0, place < total - 1
+
+    @pl.when(has_below)
+    def _():
+        pl.semaphore_signal(barrier, inc=1, device_id=neighbour(-1, across), device_id_type=MESH)
+
+    @pl.when(has_above)
+    def _():
+        pl.semaphore_signal(barrier, inc=1, device_id=neighbour(1, across), device_id_type=MESH)
+
     sources = (
+        moved_hbm,
+        points_hbm,
         modulus_hbm,
         pick_hbm,
         strain_hbm,
@@ -278,6 +308,8 @@
         force_hbm,
     )
     targets = (
+        moved_ref,
+        points_ref,
         modulus_ref,
         pick_tab,
         strain_tab,
@@ -297,8 +329,41 @@
     ]
     for load in loads:
         load.start()
-    for load in loads[:3]:
+
+    loads[0].wait()
+    sent[...] = jnp.zeros_like(sent)
+    for i in range(3):
+        sent[i : i + 1, 0:NODES] = moved_ref[i, layers - 1 : layers, :]
+    upward = pltpu.make_async_remote_copy(
+        src_ref=sent,
+        dst_ref=landed_up,
+        send_sem=send_sems.at[0],
+        recv_sem=recv_sems.at[0],
+        device_id=neighbour(1, across),
+        device_id_type=MESH,
+    )
+
+    pl.semaphore_wait(barrier, jnp.minimum(place, 1) + jnp.minimum(total - 1 - place, 1))
+
+    @pl.when(has_above)
+    def _():
+        upward.start()
+
+    nodes_ref[...] = jnp.zeros_like(nodes_ref)
+    for z in range(layers):
+        for cz in range(2):
+            for i in range(3):
+                if z + cz > 0:
+                    row = z * 8 + cz * 3 + i
+                    nodes_ref[row : row + 1, 0:NODES] = moved_ref[i, z + cz - 1 : z + cz, :]
+    for load in loads[1:5]:
         load.wait()
+
+    @pl.when(has_below)
+    def _():
+        upward.wait_recv()
+        nodes_ref[0:3, :] = landed_up[0:3, :]
+
     elems = layers * EXY * EXY
     chunks = slots // ROWS
     count = count_ref[0]
@@ -352,7 +417,7 @@
         upper = jnp.where((lane32 == k) | (lane32 == 12 + k), high, upper)
         upper = jnp.where(lane32 == 6 + k, mean_law[k] - high, upper)
     mean_parts = upper.astype(bf16)
-    for load in loads[3:5]:
+    for load in loads[5:7]:
         load.wait()
     for r in range(chunks):
         rows = slice(r * ROWS, (r + 1) * ROWS)
@@ -406,7 +471,7 @@
                     field[k * CELL + x, r * ROWS : (r + 1) * ROWS, lanes] = base - values[x]
         return carry
 
-    for load in loads[5:]:
+    for load in loads[7:]:
         load.wait()
     lax.fori_loop(0, 7, first_c, 0)
     lax.fori_loop(0, 2, first_r, 0)
@@ -524,20 +589,56 @@
         ],
         axis=0,
     )
-    force_ref[...] = total3(
+    forces[...] = total3(
         lax.dot_general(
             parts3(by_layer), pick_tab[...], (((1,), (1,)), ((), ())), preferred_element_type=f32
         )
     )
+
+    downward = pltpu.make_async_remote_copy(
+        src_ref=forces.at[0:8],
+        dst_ref=landed_down,
+        send_sem=send_sems.at[1],
+        recv_sem=recv_sems.at[1],
+        device_id=neighbour(-1, across),
+        device_id_type=MESH,
+    )
+
+    @pl.when(has_below)
+    def _():
+        downward.start()
+
+    force_ref[...] = jnp.zeros_like(force_ref)
+    for z in range(layers):
+        for i in range(3):
+            value = forces[z * 8 + 3 + i : z * 8 + 4 + i, :]
+            if z + 1 < layers:
+                value = value + forces[z * 8 + 8 + i : z * 8 + 9 + i, :]
+            force_ref[i * layers + z : i * layers + z + 1, :] = value
     for store in stores:
         store.wait()
 
-
-def run_kernel(count, nodes, modulus, points, damage, voxel, layers, interpret=False):
+    @pl.when(has_above)
+    def _():
+        downward.wait_recv()
+        for i in range(3):
+            row = i * layers + layers - 1
+            force_ref[row : row + 1, :] = force_ref[row : row + 1, :] + landed_down[i : i + 1, :]
+        upward.wait_send()
+
+    @pl.when(has_below)
+    def _():
+        downward.wait_send()
+
+
+def run_kernel(count, moved, modulus, points, damage, voxel, line):
     slots = damage.shape[0]
+    layers = moved.shape[1]
     to_strain, to_force, pick = macro_tables()
     coefs, first, forward, inverse, real_forward, real_inverse = cell_tables()
     operands = (
+        moved,
+        points,
         modulus,
         jnp.asarray(pick, bf16),
         jnp.asarray(to_strain, f32),
@@ -551,20 +652,20 @@
         jnp.asarray(coefs, f32),
         jnp.asarray(to_force, f32),
     )
-    vmem, anywhere = pl.BlockSpec(memory_space=pltpu.VMEM), pl.BlockSpec(memory_space=pl.ANY)
+    vmem, hbm = pl.BlockSpec(memory_space=pltpu.VMEM), pl.BlockSpec(memory_space=pltpu.HBM)
     rows = 6 * slots
 
     def body(*refs):
-        kernel(layers, slots, *refs)
+        kernel(layers, slots, *line, *refs)
 
     return pl.pallas_call(
         body,
         out_shape=(
-            jax.ShapeDtypeStruct((layers * 8, NODE_PAD), f32),
+            jax.ShapeDtypeStruct((layers * 4, NODE_PAD), f32),
             jax.ShapeDtypeStruct(damage.shape, bf16),
         ),
-        in_specs=[pl.BlockSpec(memory_space=pltpu.SMEM), vmem, vmem] + [anywhere] * 12,
-        out_specs=(vmem, anywhere),
+        in_specs=[pl.BlockSpec(memory_space=pltpu.SMEM)] + [hbm] * len(operands),
+        out_specs=(vmem, hbm),
         scratch_shapes=[
             pltpu.VMEM((6 * CELL, slots, PLANE), f32),
             pltpu.VMEM((7, rows, 2 * PLANE), bf16),
@@ -577,141 +678,38 @@
             pltpu.VMEM((48, layers * EXY * EXY), f32),
             pltpu.VMEM((6, slots, HALF), f32),
             pltpu.VMEM(damage.shape, bf16),
+            pltpu.VMEM((layers * 8, NODE_PAD), f32),
+            pltpu.VMEM((layers * 8, NODE_PAD), f32),
         ]
+        + [pltpu.VMEM((8, NODE_PAD), f32)] * 3
         + [pltpu.VMEM(operand.shape, operand.dtype) for operand in operands]
         + [
             pltpu.SemaphoreType.DMA((len(operands),)),
             pltpu.SemaphoreType.DMA((slots // ROWS,)),
+            pltpu.SemaphoreType.DMA((2,)),
+            pltpu.SemaphoreType.DMA((2,)),
         ],
-        compiler_params=pltpu.CompilerParams(vmem_limit_bytes=44 * 1024 * 1024),
+        compiler_params=pltpu.CompilerParams(
+            vmem_limit_bytes=44 * 1024 * 1024, collective_id=0, has_side_effects=True
+        ),
         cost_estimate=pl.CostEstimate(flops=10**10, bytes_accessed=8 * 10**6, transcendentals=0),
-        interpret=interpret,
-    )(count, nodes, points, *operands)
-
-
-def neighbour(steps, across):
-    place = lax.axis_index("dom") * across + lax.axis_index("sub") + steps
-    return (place // across, place % across)
-
-
-def spread_kernel(layers, total, across, moved_ref, nodes_ref, sent, landed, send_sem, recv_sem):
-    place = lax.axis_index("dom") * across + lax.axis_index("sub")
-    barrier = pltpu.get_barrier_semaphore()
-
-    @pl.when(place > 0)
-    def _():
-        pl.semaphore_signal(
-            barrier, inc=1, device_id=neighbour(-1, across), device_id_type=MESH
-        )
-
-    sent[...] = jnp.zeros_like(sent)
-    for i in range(3):
-        sent[i : i + 1, 0:NODES] = moved_ref[i, layers - 1 : layers, :]
-    copy = pltpu.make_async_remote_copy(
-        src_ref=sent,
-        dst_ref=landed,
-        send_sem=send_sem,
-        recv_sem=recv_sem,
-        device_id=neighbour(1, across),
-        device_id_type=MESH,
-    )
-
-    @pl.when(place < total - 1)
-    def _():
-        pl.semaphore_wait(barrier, 1)
-        copy.start()
-
-    nodes_ref[...] = jnp.zeros_like(nodes_ref)
-    for z in range(layers):
-        for cz in range(2):
-            for i in range(3):
-                if z + cz > 0:
-                    row = z * 8 + cz * 3 + i
-                    nodes_ref[row : row + 1, 0:NODES] = moved_ref[i, z + cz - 1 : z + cz, :]
-
-    @pl.when(place > 0)
-    def _():
-        copy.wait_recv()
-        nodes_ref[0:3, :] = landed[0:3, :]
-
-    @pl.when(place < total - 1)
-    def _():
-        copy.wait_send()
-
-
-def gather_kernel(layers, total, across, force_ref, out_ref, landed, send_sem, recv_sem):
-    place = lax.axis_index("dom") * across + lax.axis_index("sub")
-    barrier = pltpu.get_barrier_semaphore()
-
-    @pl.when(place < total - 1)
-    def _():
-        pl.semaphore_signal(
-            barrier, inc=1, device_id=neighbour(1, across), device_id_type=MESH
-        )
-
-    copy = pltpu.make_async_remote_copy(
-        src_ref=force_ref.at[0:8],
-        dst_ref=landed,
-        send_sem=send_sem,
-        recv_sem=recv_sem,
-        device_id=neighbour(-1, across),
-        device_id_type=MESH,
-    )
-
-    @pl.when(place > 0)
-    def _():
-        pl.semaphore_wait(barrier, 1)
-        copy.start()
-
-    for z in range(layers):
-        for i in range(3):
-            value = force_ref[z * 8 + 3 + i : z * 8 + 4 + i, 0:NODES]
-            if z + 1 < layers:
-                value = value + force_ref[z * 8 + 8 + i : z * 8 + 9 + i, 0:NODES]
-            out_ref[i, z : z + 1, :] = value
-
-    @pl.when(place < total - 1)
-    def _():
-        copy.wait_recv()
-        for i in range(3):
-            out_ref[i, layers - 1 : layers, :] += landed[i : i + 1, 0:NODES]
-
-    @pl.when(place > 0)
-    def _():
-        copy.wait_send()
-
-
-def exchange(function, value, shape, scratch, collective_id):
-    vmem = pl.BlockSpec(memory_space=pltpu.VMEM)
-    tile = pltpu.VMEM((8, NODE_PAD), f32)
-    return pl.pallas_call(
-        function,
-        out_shape=jax.ShapeDtypeStruct(shape, f32),
-        in_specs=[vmem],
-        out_specs=vmem,
-        scratch_shapes=[tile] * scratch + [pltpu.SemaphoreType.DMA] * 2,
-        compiler_params=pltpu.CompilerParams(collective_id=collective_id, has_side_effects=True),
-    )(value)
+    )(count, *operands)
 
 
 def body(displacement, macro_modulus, damaged_count, damaged_points, damage, voxel_modulus):
     layers = displacement.shape[1]
     across = lax.axis_size("sub")
     total = lax.axis_size("dom") * across
-    nodes = exchange(
-        functools.partial(spread_kernel, layers, total, across),
+    force, new_damage = run_kernel(
+        damaged_count,
         displacement,
-        (layers * 8, NODE_PAD),
-        2,
-        0,
-    )
-    force, new_damage = run_kernel(
-        damaged_count, nodes, macro_modulus, damaged_points, damage, voxel_modulus, layers
-    )
-    own_forces = exchange(
-        functools.partial(gather_kernel, layers, total, across), force, displacement.shape, 1, 1
-    )
-    return (own_forces, new_damage)
+        macro_modulus,
+        damaged_points,
+        damage,
+        voxel_modulus,
+        (total, across),
+    )
+    return (force[: 3 * layers].reshape(3, layers, NODE_PAD)[:, :, :NODES], new_damage)
 
 
 def solution(mesh):

time: 47.9 us -> 45.8 us (0.956)
  Pallas kernels: 33.8 us -> 30.9 us
  local copies, waits for them, and re-layouts: 12 us -> 12.9 us
    pallas_call x3 -> x1, Pallas kernels: 33.8 us -> 30.9 us  [run_kernel(): pl.pallas_call(body, out_shape=(jax.ShapeDtypeStruct((layers * 4, NODE_PA...]
    reshape x0 -> x1, local copies, waits for them, and re-layouts: none -> 0.62 us  [body(): force[:3 * layers].reshape(3, layers, NODE_PAD)[:, :, :NODES]]
    unnamed x31 -> x29, local copies, waits for them, and re-layouts: 12 us -> 12.3 us
where the time goes in v2:
time: 45.8 us; the launch traced here: 45.1 us
  Pallas kernels  30.9 us (67%)
  local copies, waits for them, and re-layouts  12.9 us (28%)
  between operations  1.33 us (3%)
    pallas_call x1, Pallas kernels, run_kernel(): pl.pallas_call(body, out_shape=(jax.ShapeDtypeStruct((layers * 4, NODE_PA...  30.9 us
    unnamed x29, local copies, waits for them, and re-layouts  12.3 us

profile of v2, /device:TPU:23, one launch (start us, length us, event | category | flops | bytes accessed | tf_op | source)
XLA Modules:
  0.0 45.1 jit_solution(16249835286185501855)
XLA Ops:
  0.6 0.0 copy-start.13
  0.6 0.0 copy-start.4
  1.3 0.0 copy-done.13
  1.4 0.0 copy-done.4
  1.4 0.0 copy-start
  1.4 1.0 %copy-done = bf16[64,4096]{1,0:T(8,128)(2,1)S(1)} copy-done((bf16[64,4096]{1,0:T(8,128)(2,1)S(1)}, bf16[64,4096]{1,0:T(8,128)(2,1)}, u32[]{:S(2)}) %copy-start) | copy-done | bytes 524312
  2.4 0.0 copy-start.1
  2.4 1.0 %copy-done.1 = bf16[64,4096]{1,0:T(8,128)(2,1)S(1)} copy-done((bf16[64,4096]{1,0:T(8,128)(2,1)S(1)}, bf16[64,4096]{1,0:T(8,128)(2,1)}, u32[]{:S(2)}) %copy-start.1) | copy-done | bytes 524312
  3.4 0.0 copy-start.2
  3.4 0.8 %copy-done.2 = f32[8,1024]{1,0:T(8,128)S(1)} copy-done((f32[8,1024]{1,0:T(8,128)S(1)}, f32[8,1024]{1,0:T(8,128)}, u32[]{:S(2)}) %copy-start.2) | copy-done | bytes 32792
  4.2 0.0 copy-start.3
  4.2 0.7 %copy-done.3 = f32[3,4,289]{2,1,0:T(4,128)S(1)} copy-done((f32[3,4,289]{2,1,0:T(4,128)S(1)}, f32[3,4,289]{2,1,0:T(4,128)}, u32[]{:S(2)}) %copy-start.3) | copy-done | bytes 13896
  4.9 0.0 copy-start.5
  4.9 1.2 %copy-done.5 = bf16[9,32,1536]{2,1,0:T(8,128)(2,1)S(1)} copy-done((bf16[9,32,1536]{2,1,0:T(8,128)(2,1)S(1)}, bf16[9,32,1536]{2,1,0:T(8,128)(2,1)}, u32[]{:S(2)}) %copy-start.5) | copy-done | bytes 884760
  6.1 1.1 %copy-done.6 = bf16[384,1024]{1,0:T(8,128)(2,1)S(1)} copy-done((bf16[384,1024]{1,0:T(8,128)(2,1)S(1)}, bf16[384,1024]{1,0:T(8,128)(2,1)}, u32[]{:S(2)}) %copy-start.6) | copy-done | bytes 786456
  7.2 1.0 %copy-done.7 = bf16[512,512]{1,0:T(8,128)(2,1)S(1)} copy-done((bf16[512,512]{1,0:T(8,128)(2,1)S(1)}, bf16[512,512]{1,0:T(8,128)(2,1)}, u32[]{:S(2)}) %copy-start.7) | copy-done | bytes 524312
  8.3 1.0 %copy-done.8 = bf16[512,512]{1,0:T(8,128)(2,1)S(1)} copy-done((bf16[512,512]{1,0:T(8,128)(2,1)S(1)}, bf16[512,512]{1,0:T(8,128)(2,1)}, u32[]{:S(2)}) %copy-start.8) | copy-done | bytes 524312
  9.3 0.9 %copy-done.9 = f32[9,24,256]{2,1,0:T(8,128)S(1)} copy-done((f32[9,24,256]{2,1,0:T(8,128)S(1)}, f32[9,24,256]{2,1,0:T(8,128)}, u32[]{:S(2)}) %copy-start.9) | copy-done | bytes 221208
  10.2 0.9 %copy-done.10 = bf16[256,256]{1,0:T(8,128)(2,1)S(1)} copy-done((bf16[256,256]{1,0:T(8,128)(2,1)S(1)}, bf16[256,256]{1,0:T(8,128)(2,1)}, u32[]{:S(2)}) %copy-start.10) | copy-done | bytes 131096
  11.2 0.9 %copy-done.11 = bf16[256,256]{1,0:T(8,128)(2,1)S(1)} copy-done((bf16[256,256]{1,0:T(8,128)(2,1)S(1)}, bf16[256,256]{1,0:T(8,128)(2,1)}, u32[]{:S(2)}) %copy-start.11) | copy-done | bytes 131096
  12.1 0.7 %copy-done.12 = f32[48,32]{1,0:T(8,128)S(1)} copy-done((f32[48,32]{1,0:T(8,128)S(1)}, f32[48,32]{1,0:T(8,128)}, u32[]{:S(2)}) %copy-start.12) | copy-done | bytes 6168
  12.8 30.9 %shard_map.158 = (f32[16,384]{1,0:T(8,128)S(1)}, bf16[64,4096]{1,0:T(8,128)(2,1)S(1)}) custom-call(s32[1]{0:T(128)S(6)} %copy.18.refs_0_, f32[3,4,289]{2,1,0:T(4,128)S(1)} %copy-done.3, s32[1,64]{1,0:T(1,128)S(1)} %copy-done.4, f32[8,1024]{1,0:T(8,128)S(1)} %copy-done.2, bf16[384,1024]{1,0:T(8,128)(2,1)S(1)} %copy-done.6, f32[48,32]{1,0:T(8,128)S(1)} %copy-done.12, ...), custom_call_target="tpu_custom_call" | custom-call | flops 10000000000 | bytes 8000000 | tf_op jit(solution)/shard_map/pallas_call | solution.py:661
  43.7 0.6 %reshape.7 = f32[3,4,384]{2,1,0:T(4,128)} reshape(f32[12,384]{1,0:T(8,128)S(1)} %bitcast.2) | data formatting | bytes 36864 | tf_op jit(solution)/shard_map/reshape | solution.py:712
  44.3 0.8 %copy.19 = bf16[64,4096]{1,0:T(8,128)(2,1)} copy(bf16[64,4096]{1,0:T(8,128)(2,1)S(1)} %get-tuple-element.9) | data formatting | bytes 1048576
  (7 shorter events, 0.0 us)
Async XLA Ops:
  0.6 0.7 %copy-start.13 = (f32[32,48]{1,0:T(8,128)S(1)}, f32[32,48]{1,0:T(8,128)}, u32[]{:S(2)}) copy-start(f32[32,48]{1,0:T(8,128)} %constant.26.clone.refs_14_) | copy-start | bytes 18436
  0.6 0.7 %copy-start.4 = (s32[1,64]{1,0:T(1,128)S(1)}, s32[1,64]{1,0:T(1,128)}, u32[]{:S(2)}) copy-start(s32[1,64]{1,0:T(1,128)} %refs_2_.1) | copy-start | bytes 772
  1.4 1.0 %copy-start = (bf16[64,4096]{1,0:T(8,128)(2,1)S(1)}, bf16[64,4096]{1,0:T(8,128)(2,1)}, u32[]{:S(2)}) copy-start(bf16[64,4096]{1,0:T(8,128)(2,1)} %refs_6_.1) | copy-start | bytes 1572868
  2.4 1.0 %copy-start.1 = (bf16[64,4096]{1,0:T(8,128)(2,1)S(1)}, bf16[64,4096]{1,0:T(8,128)(2,1)}, u32[]{:S(2)}) copy-start(bf16[64,4096]{1,0:T(8,128)(2,1)} %refs_7_.1) | copy-start | bytes 1572868
  3.4 0.8 %copy-start.2 = (f32[8,1024]{1,0:T(8,128)S(1)}, f32[8,1024]{1,0:T(8,128)}, u32[]{:S(2)}) copy-start(f32[8,1024]{1,0:T(8,128)} %refs_3_.1) | copy-start | bytes 98308
  4.2 0.7 %copy-start.3 = (f32[3,4,289]{2,1,0:T(4,128)S(1)}, f32[3,4,289]{2,1,0:T(4,128)}, u32[]{:S(2)}) copy-start(f32[3,4,289]{2,1,0:T(4,128)} %refs_1_.1) | copy-start | bytes 41620
  4.9 1.2 %copy-start.5 = (bf16[9,32,1536]{2,1,0:T(8,128)(2,1)S(1)}, bf16[9,32,1536]{2,1,0:T(8,128)(2,1)}, u32[]{:S(2)}) copy-start(bf16[9,32,1536]{2,1,0:T(8,128)(2,1)} %constant.21.clone.refs_9_) | copy-start | bytes 2654212
  6.1 1.1 %copy-start.6 = (bf16[384,1024]{1,0:T(8,128)(2,1)S(1)}, bf16[384,1024]{1,0:T(8,128)(2,1)}, u32[]{:S(2)}) copy-start(bf16[384,1024]{1,0:T(8,128)(2,1)} %constant.18.clone.refs_4_) | copy-start | bytes 2359300
  7.2 1.0 %copy-start.7 = (bf16[512,512]{1,0:T(8,128)(2,1)S(1)}, bf16[512,512]{1,0:T(8,128)(2,1)}, u32[]{:S(2)}) copy-start(bf16[512,512]{1,0:T(8,128)(2,1)} %constant.22.clone.refs_10_) | copy-start | bytes 1572868
  8.3 1.0 %copy-start.8 = (bf16[512,512]{1,0:T(8,128)(2,1)S(1)}, bf16[512,512]{1,0:T(8,128)(2,1)}, u32[]{:S(2)}) copy-start(bf16[512,512]{1,0:T(8,128)(2,1)} %constant.20.clone.refs_8_) | copy-start | bytes 1572868
  9.3 0.9 %copy-start.9 = (f32[9,24,256]{2,1,0:T(8,128)S(1)}, f32[9,24,256]{2,1,0:T(8,128)}, u32[]{:S(2)}) copy-start(f32[9,24,256]{2,1,0:T(8,128)} %constant.25.clone.refs_13_) | copy-start | bytes 663556
  10.2 0.9 %copy-start.10 = (bf16[256,256]{1,0:T(8,128)(2,1)S(1)}, bf16[256,256]{1,0:T(8,128)(2,1)}, u32[]{:S(2)}) copy-start(bf16[256,256]{1,0:T(8,128)(2,1)} %constant.24.clone.refs_12_) | copy-start | bytes 393220
  11.1 0.9 %copy-start.11 = (bf16[256,256]{1,0:T(8,128)(2,1)S(1)}, bf16[256,256]{1,0:T(8,128)(2,1)}, u32[]{:S(2)}) copy-start(bf16[256,256]{1,0:T(8,128)(2,1)} %constant.23.clone.refs_11_) | copy-start | bytes 393220
  12.1 0.7 %copy-start.12 = (f32[48,32]{1,0:T(8,128)S(1)}, f32[48,32]{1,0:T(8,128)}, u32[]{:S(2)}) copy-start(f32[48,32]{1,0:T(8,128)} %constant.19.clone.refs_5_) | copy-start | bytes 18436

commit v3 on v2

--- a/solution.py
+++ b/solution.py
@@ -446,7 +446,8 @@
             rows = slice(k * slots, (k + 1) * slots)
             green[rows, 0:PLANE] = (part * spectrum[:, 0:PLANE]).astype(bf16)
             green[rows, PLANE:] = (part * spectrum[:, PLANE:]).astype(bf16)
-        back_c[j] = jnp.dot(green[...], inverse_tab[...], preferred_element_type=f32)
+        wave = jnp.dot(green[...], inverse_tab[...], preferred_element_type=f32)
+        back_c[j] = wave.astype(bf16)
         return carry
 
     def first_r(j, carry):
@@ -455,7 +456,8 @@
         for k in range(6):
             part = weight[:, k * PLANE : (k + 1) * PLANE]
             green[k * slots : (k + 1) * slots, 0:PLANE] = (part * spectrum).astype(bf16)
-        back_r[j] = jnp.dot(green[:, 0:PLANE], real_inverse[...], preferred_element_type=f32)
+        wave = jnp.dot(green[:, 0:PLANE], real_inverse[...], preferred_element_type=f32)
+        back_r[j] = wave.astype(bf16)
         return carry
 
     def to_strain(k, carry):
@@ -468,7 +470,9 @@
                 pairs = [(back_c[j, rows, lanes], back_c[j, rows, upper_lanes]) for j in range(7)]
                 values = inverse_x(back_r[0, rows, lanes], back_r[1, rows, lanes], pairs)
                 for x in range(CELL):
-                    field[k * CELL + x, r * ROWS : (r + 1) * ROWS, lanes] = base - values[x]
+                    field[k * CELL + x, r * ROWS : (r + 1) * ROWS, lanes] = (
+                        base - values[x].astype(f32)
+                    )
         return carry
 
     for load in loads[7:]:
@@ -509,7 +513,7 @@
         for h in range(2):
             lanes = slice(h * HALF, (h + 1) * HALF)
             coefs = [
-                jnp.broadcast_to(coef_tab[index, c : c + 1, lanes], (ROWS, HALF))
+                jnp.broadcast_to(coef_tab[index, c : c + 1, lanes], (ROWS, HALF)).astype(bf16)
                 for c in range(21)
             ]
             for part in range(planes):
@@ -523,20 +527,22 @@
                         total = coefs[packed[(k, 0)]] * t[0]
                         for b in range(1, 6):
                             total = total + coefs[packed[(k, b)]] * t[b]
-                        green[k * slots + r * ROWS : k * slots + (r + 1) * ROWS, where] = (
-                            total.astype(bf16)
-                        )
+                        green[k * slots + r * ROWS : k * slots + (r + 1) * ROWS, where] = total
 
     def second_c(j, carry):
-        freq[...] = jnp.dot(spec_c[j], forward_tab[...], preferred_element_type=f32)
+        spectrum = jnp.dot(spec_c[j], forward_tab[...], preferred_element_type=f32)
+        freq[...] = spectrum.astype(bf16)
         apply_green(j + 1, 2)
-        back_c[j] = jnp.dot(green[...], inverse_tab[...], preferred_element_type=f32)
+        wave = jnp.dot(green[...], inverse_tab[...], preferred_element_type=f32)
+        back_c[j] = wave.astype(bf16)
         return carry
 
     def second_r(j, carry):
-        freq[:, 0:PLANE] = jnp.dot(spec_r[j], real_forward[...], preferred_element_type=f32)
+        spectrum = jnp.dot(spec_r[j], real_forward[...], preferred_element_type=f32)
+        freq[:, 0:PLANE] = spectrum.astype(bf16)
         apply_green(j * 8, 1)
-        back_r[j] = jnp.dot(green[:, 0:PLANE], real_inverse[...], preferred_element_type=f32)
+        wave = jnp.dot(green[:, 0:PLANE], real_inverse[...], preferred_element_type=f32)
+        back_r[j] = wave.astype(bf16)
         return carry
 
     lax.fori_loop(0, CELL, polarize, 0)
@@ -670,9 +676,9 @@
             pltpu.VMEM((6 * CELL, slots, PLANE), f32),
             pltpu.VMEM((7, rows, 2 * PLANE), bf16),
             pltpu.VMEM((2, rows, PLANE), bf16),
-            pltpu.VMEM((7, rows, 2 * PLANE), f32),
-            pltpu.VMEM((2, rows, PLANE), f32),
-            pltpu.VMEM((rows, 2 * PLANE), f32),
+            pltpu.VMEM((7, rows, 2 * PLANE), bf16),
+            pltpu.VMEM((2, rows, PLANE), bf16),
+            pltpu.VMEM((rows, 2 * PLANE), bf16),
             pltpu.VMEM((rows, 2 * PLANE), bf16),
             pltpu.VMEM((6, slots, HALF), f32),
             pltpu.VMEM((48, layers * EXY * EXY), f32),
@@ -690,7 +696,7 @@
             pltpu.SemaphoreType.DMA((2,)),
         ],
         compiler_params=pltpu.CompilerParams(
-            vmem_limit_bytes=44 * 1024 * 1024, collective_id=0, has_side_effects=True
+            vmem_limit_bytes=65500 * 1024, collective_id=0, has_side_effects=True
         ),
         cost_estimate=pl.CostEstimate(flops=10**10, bytes_accessed=8 * 10**6, transcendentals=0),
     )(count, *operands)

time: 45.8 us -> 34.9 us (0.76)
  local copies, waits for them, and re-layouts: 12.9 us -> 3.22 us
  Pallas kernels: 30.9 us -> 30.1 us
    unnamed x29 -> x1, local copies, waits for them, and re-layouts: 12.3 us -> 1.87 us
    pallas_call x1, Pallas kernels: 30.9 us -> 30.1 us  [run_kernel(): pl.pallas_call(body, out_shape=(jax.ShapeDtypeStruct((layers * 4, NODE_PA...]
    reshape x1, local copies, waits for them, and re-layouts: 0.62 us -> 1.35 us  [body(): force[:3 * layers].reshape(3, layers, NODE_PAD)[:, :, :NODES]]
where the time goes in v3:
time: 34.9 us; the launch traced here: 34.6 us
  Pallas kernels  30.1 us (86%)
  local copies, waits for them, and re-layouts  3.22 us (9%)
  between operations  1.29 us (4%)
    pallas_call x1, Pallas kernels, run_kernel(): pl.pallas_call(body, out_shape=(jax.ShapeDtypeStruct((layers * 4, NODE_PA...  30.1 us
    unnamed x1, local copies, waits for them, and re-layouts  1.87 us
    reshape x1, local copies, waits for them, and re-layouts, body(): force[:3 * layers].reshape(3, layers, NODE_PAD)[:, :, :NODES]  1.35 us

profile of v3, /device:TPU:23, one launch (start us, length us, event | category | flops | bytes accessed | tf_op | source)
XLA Modules:
  0.0 34.6 jit_solution(15620200047359231490)
XLA Ops:
  1.3 30.1 %shard_map.158 = (f32[16,384]{1,0:T(8,128)}, bf16[64,4096]{1,0:T(8,128)(2,1)}) custom-call(s32[1]{0:T(128)S(6)} %copy.18.refs_0_, f32[3,4,289]{2,1,0:T(4,128)} %refs_1_.1, s32[1,64]{1,0:T(1,128)} %refs_2_.1, f32[8,1024]{1,0:T(8,128)} %refs_3_.1, bf16[384,1024]{1,0:T(8,128)(2,1)} %constant.18.clone.refs_4_, f32[48,32]{1,0:T(8,128)} %constant.19.clone.refs_5_, ...), custom_call_target="tpu_custom_call" | custom-call | flops 10000000000 | bytes 8000000 | tf_op jit(solution)/shard_map/pallas_call | solution.py:667
  31.4 1.4 %reshape.7 = f32[3,4,384]{2,1,0:T(4,128)} reshape(f32[12,384]{1,0:T(8,128)} %bitcast.2) | data formatting | bytes 36864 | tf_op jit(solution)/shard_map/reshape | solution.py:718
  32.8 1.9 %copy.19 = bf16[64,4096]{1,0:T(8,128)(2,1)} copy(bf16[64,4096]{1,0:T(8,128)(2,1)} %get-tuple-element.9) | data formatting | bytes 1048576

commit v4 on v3

--- a/solution.py
+++ b/solution.py
@@ -438,27 +438,31 @@
                     bf16
                 )
 
-    def first_c(j, carry):
-        spectrum = jnp.dot(spec_c[j, 0:slots], forward_tab[...], preferred_element_type=f32)
-        weight = jnp.dot(mean_parts, first_tab[j + 1], preferred_element_type=f32)
+    waves = [(spec_c, back_c, j, j + 1, 2) for j in range(7)]
+    waves += [(spec_r, back_r, j, j * 8, 1) for j in range(2)]
+
+    def forward_yz(wave, rows):
+        spec, _, j, _, planes = waves[wave]
+        table = forward_tab if planes == 2 else real_forward
+        return jnp.dot(spec[j, 0:rows], table[...], preferred_element_type=f32)
+
+    def inverse_yz(wave):
+        _, back, j, _, planes = waves[wave]
+        table = inverse_tab if planes == 2 else real_inverse
+        value = green[wave % 2, :, 0 : planes * PLANE]
+        back[j] = jnp.dot(value, table[...], preferred_element_type=f32).astype(bf16)
+
+    def first_green(wave):
+        index, planes = waves[wave][3:]
+        spectrum = forward_yz(wave, slots)
+        weight = jnp.dot(mean_parts, first_tab[index], preferred_element_type=f32)
         for k in range(6):
             part = weight[:, k * PLANE : (k + 1) * PLANE]
-            rows = slice(k * slots, (k + 1) * slots)
-            green[rows, 0:PLANE] = (part * spectrum[:, 0:PLANE]).astype(bf16)
-            green[rows, PLANE:] = (part * spectrum[:, PLANE:]).astype(bf16)
-        wave = jnp.dot(green[...], inverse_tab[...], preferred_element_type=f32)
-        back_c[j] = wave.astype(bf16)
-        return carry
-
-    def first_r(j, carry):
-        spectrum = jnp.dot(spec_r[j, 0:slots], real_forward[...], preferred_element_type=f32)
-        weight = jnp.dot(mean_parts, first_tab[j * 8], preferred_element_type=f32)
-        for k in range(6):
-            part = weight[:, k * PLANE : (k + 1) * PLANE]
-            green[k * slots : (k + 1) * slots, 0:PLANE] = (part * spectrum).astype(bf16)
-        wave = jnp.dot(green[:, 0:PLANE], real_inverse[...], preferred_element_type=f32)
-        back_r[j] = wave.astype(bf16)
-        return carry
+            for plane_no in range(planes):
+                lanes = slice(plane_no * PLANE, (plane_no + 1) * PLANE)
+                green[wave % 2, k * slots : (k + 1) * slots, lanes] = (
+                    part * spectrum[:, lanes]
+                ).astype(bf16)
 
     def to_strain(k, carry):
         for r in range(chunks):
@@ -477,8 +481,11 @@
 
     for load in loads[7:]:
         load.wait()
-    lax.fori_loop(0, 7, first_c, 0)
-    lax.fori_loop(0, 2, first_r, 0)
+    first_green(0)
+    for wave in range(9):
+        if wave < 8:
+            first_green(wave + 1)
+        inverse_yz(wave)
     lax.fori_loop(0, 6, to_strain, 0)
 
     def polarize(x, carry):
@@ -509,7 +516,9 @@
                     spec_c[j, rows, upper_lanes] = pairs[j][1].astype(bf16)
         return carry
 
-    def apply_green(index, planes):
+    def apply_green(wave):
+        index, planes = waves[wave][3:]
+        half = wave % 2
         for h in range(2):
             lanes = slice(h * HALF, (h + 1) * HALF)
             coefs = [
@@ -520,35 +529,29 @@
                 where = slice(part * PLANE + h * HALF, part * PLANE + (h + 1) * HALF)
                 for r in range(chunks):
                     t = [
-                        freq[k * slots + r * ROWS : k * slots + (r + 1) * ROWS, where]
+                        freq[half, k * slots + r * ROWS : k * slots + (r + 1) * ROWS, where]
                         for k in range(6)
                     ]
                     for k in range(6):
                         total = coefs[packed[(k, 0)]] * t[0]
                         for b in range(1, 6):
                             total = total + coefs[packed[(k, b)]] * t[b]
-                        green[k * slots + r * ROWS : k * slots + (r + 1) * ROWS, where] = total
-
-    def second_c(j, carry):
-        spectrum = jnp.dot(spec_c[j], forward_tab[...], preferred_element_type=f32)
-        freq[...] = spectrum.astype(bf16)
-        apply_green(j + 1, 2)
-        wave = jnp.dot(green[...], inverse_tab[...], preferred_element_type=f32)
-        back_c[j] = wave.astype(bf16)
-        return carry
-
-    def second_r(j, carry):
-        spectrum = jnp.dot(spec_r[j], real_forward[...], preferred_element_type=f32)
-        freq[:, 0:PLANE] = spectrum.astype(bf16)
-        apply_green(j * 8, 1)
-        wave = jnp.dot(green[:, 0:PLANE], real_inverse[...], preferred_element_type=f32)
-        back_r[j] = wave.astype(bf16)
-        return carry
+                        green[half, k * slots + r * ROWS : k * slots + (r + 1) * ROWS, where] = (
+                            total
+                        )
+
+    def second_spectrum(wave):
+        lanes = waves[wave][4] * PLANE
+        freq[wave % 2, :, 0:lanes] = forward_yz(wave, 6 * slots).astype(bf16)
 
     lax.fori_loop(0, CELL, polarize, 0)
     lax.fori_loop(0, 6, to_spectrum, 0)
-    lax.fori_loop(0, 7, second_c, 0)
-    lax.fori_loop(0, 2, second_r, 0)
+    second_spectrum(0)
+    for wave in range(9):
+        if wave < 8:
+            second_spectrum(wave + 1)
+        apply_green(wave)
+        inverse_yz(wave)
     lax.fori_loop(0, 6, to_strain, 0)
 
     stores = []
@@ -678,8 +681,8 @@
             pltpu.VMEM((2, rows, PLANE), bf16),
             pltpu.VMEM((7, rows, 2 * PLANE), bf16),
             pltpu.VMEM((2, rows, PLANE), bf16),
-            pltpu.VMEM((rows, 2 * PLANE), bf16),
-            pltpu.VMEM((rows, 2 * PLANE), bf16),
+            pltpu.VMEM((2, rows, 2 * PLANE), bf16),
+            pltpu.VMEM((2, rows, 2 * PLANE), bf16),
             pltpu.VMEM((6, slots, HALF), f32),
             pltpu.VMEM((48, layers * EXY * EXY), f32),
             pltpu.VMEM((6, slots, HALF), f32),

time: 34.9 us -> 30.4 us (0.87)
  Pallas kernels: 30.1 us -> 25.6 us
    pallas_call x1, Pallas kernels: 30.1 us -> 25.6 us  [run_kernel(): pl.pallas_call(body, out_shape=(jax.ShapeDtypeStruct((layers * 4, NODE_PA...]
where the time goes in v4:
time: 30.4 us; the launch traced here: 30.1 us
  Pallas kernels  25.6 us (84%)
  local copies, waits for them, and re-layouts  3.22 us (11%)
  between operations  1.29 us (4%)
    pallas_call x1, Pallas kernels, run_kernel(): pl.pallas_call(body, out_shape=(jax.ShapeDtypeStruct((layers * 4, NODE_PA...  25.6 us
    unnamed x1, local copies, waits for them, and re-layouts  1.87 us
    reshape x1, local copies, waits for them, and re-layouts, body(): force[:3 * layers].reshape(3, layers, NODE_PAD)[:, :, :NODES]  1.35 us

profile of v4, /device:TPU:23, one launch (start us, length us, event | category | flops | bytes accessed | tf_op | source)
XLA Modules:
  0.0 30.1 jit_solution(1235601096321678231)
XLA Ops:
  1.3 25.6 %shard_map.158 = (f32[16,384]{1,0:T(8,128)}, bf16[64,4096]{1,0:T(8,128)(2,1)}) custom-call(s32[1]{0:T(128)S(6)} %copy.18.refs_0_, f32[3,4,289]{2,1,0:T(4,128)} %refs_1_.1, s32[1,64]{1,0:T(1,128)} %refs_2_.1, f32[8,1024]{1,0:T(8,128)} %refs_3_.1, bf16[384,1024]{1,0:T(8,128)(2,1)} %constant.18.clone.refs_4_, f32[48,32]{1,0:T(8,128)} %constant.19.clone.refs_5_, ...), custom_call_target="tpu_custom_call" | custom-call | flops 10000000000 | bytes 8000000 | tf_op jit(solution)/shard_map/pallas_call | solution.py:670
  26.9 1.4 %reshape.7 = f32[3,4,384]{2,1,0:T(4,128)} reshape(f32[12,384]{1,0:T(8,128)} %bitcast.2) | data formatting | bytes 36864 | tf_op jit(solution)/shard_map/reshape | solution.py:721
  28.3 1.9 %copy.19 = bf16[64,4096]{1,0:T(8,128)(2,1)} copy(bf16[64,4096]{1,0:T(8,128)(2,1)} %get-tuple-element.9) | data formatting | bytes 1048576

commit v5 on v4

--- a/solution.py
+++ b/solution.py
@@ -150,9 +150,9 @@
 
 def forward_x(v):
     s = [v[x] + v[x + 8] for x in range(8)]
-    d = [v[x] - v[x + 8] for x in range(8)]
+    d = [(v[x] - v[x + 8]).astype(bf16) for x in range(8)]
     a = [s[x] + s[x + 4] for x in range(4)]
-    b = [s[x] - s[x + 4] for x in range(4)]
+    b = [(s[x] - s[x + 4]).astype(bf16) for x in range(4)]
     a02, a13 = a[0] + a[2], a[1] + a[3]
     bm, bp = C2 * (b[1] - b[3]), C2 * (b[1] + b[3])
     p1, p2, p3 = d[1] - d[7], C2 * (d[2] - d[6]), d[3] - d[5]
@@ -544,7 +544,7 @@
         lanes = waves[wave][4] * PLANE
         freq[wave % 2, :, 0:lanes] = forward_yz(wave, 6 * slots).astype(bf16)
 
-    lax.fori_loop(0, CELL, polarize, 0)
+    lax.fori_loop(0, CELL, polarize, 0, unroll=2)
     lax.fori_loop(0, 6, to_spectrum, 0)
     second_spectrum(0)
     for wave in range(9):
@@ -573,7 +573,7 @@
                 out.append(sums[k] + (value[:, 0:HALF] + value[:, HALF:]))
             return tuple(out)
 
-        sums = lax.fori_loop(0, CELL, finish, (jnp.zeros((ROWS, HALF), f32),) * 6)
+        sums = lax.fori_loop(0, CELL, finish, (jnp.zeros((ROWS, HALF), f32),) * 6, unroll=4)
         for k in range(6):
             acc[k, rows] = sums[k]
         stores.append(pltpu.make_async_copy(new_ref.at[rows], new_hbm.at[rows], out_sems.at[r]))

time: 30.4 us -> 29.6 us (0.974)
  Pallas kernels: 25.6 us -> 24.9 us
    pallas_call x1, Pallas kernels: 25.6 us -> 24.9 us  [run_kernel(): pl.pallas_call(body, out_shape=(jax.ShapeDtypeStruct((layers * 4, NODE_PA...]
where the time goes in v5:
time: 29.6 us; the launch traced here: 29.4 us
  Pallas kernels  24.9 us (84%)
  local copies, waits for them, and re-layouts  3.22 us (11%)
  between operations  1.29 us (4%)
    pallas_call x1, Pallas kernels, run_kernel(): pl.pallas_call(body, out_shape=(jax.ShapeDtypeStruct((layers * 4, NODE_PA...  24.9 us
    unnamed x1, local copies, waits for them, and re-layouts  1.87 us
    reshape x1, local copies, waits for them, and re-layouts, body(): force[:3 * layers].reshape(3, layers, NODE_PAD)[:, :, :NODES]  1.35 us

profile of v5, /device:TPU:23, one launch (start us, length us, event | category | flops | bytes accessed | tf_op | source)
XLA Modules:
  0.0 29.4 jit_solution(5268942926674118843)
XLA Ops:
  1.3 24.9 %shard_map.158 = (f32[16,384]{1,0:T(8,128)}, bf16[64,4096]{1,0:T(8,128)(2,1)}) custom-call(s32[1]{0:T(128)S(6)} %copy.18.refs_0_, f32[3,4,289]{2,1,0:T(4,128)} %refs_1_.1, s32[1,64]{1,0:T(1,128)} %refs_2_.1, f32[8,1024]{1,0:T(8,128)} %refs_3_.1, bf16[384,1024]{1,0:T(8,128)(2,1)} %constant.18.clone.refs_4_, f32[48,32]{1,0:T(8,128)} %constant.19.clone.refs_5_, ...), custom_call_target="tpu_custom_call" | custom-call | flops 10000000000 | bytes 8000000 | tf_op jit(solution)/shard_map/pallas_call | solution.py:670
  26.2 1.4 %reshape.7 = f32[3,4,384]{2,1,0:T(4,128)} reshape(f32[12,384]{1,0:T(8,128)} %bitcast.2) | data formatting | bytes 36864 | tf_op jit(solution)/shard_map/reshape | solution.py:721
  27.5 1.9 %copy.19 = bf16[64,4096]{1,0:T(8,128)(2,1)} copy(bf16[64,4096]{1,0:T(8,128)(2,1)} %get-tuple-element.9) | data formatting | bytes 1048576
